TPU v7x, 32 devices: a whole 2x2x4 slice. The times are simulated.
32 devices in a mesh: dp: 8 (over z, y), ty: 2 (over core), tz: 2 (over x).
Axes of the slice: x: 2, y: 2, z: 4, core: 2. Of those that a mesh axis runs over, the one named last changes fastest.
Arguments:
- inputs: bfloat16 [8, 4, 48, 48, 256], P('dp', None, 'ty', 'tz'), may hold values from -6 to 6
- pre_first: bfloat16 [8, 4, 48, 48, 256], P('dp', None, 'ty', 'tz'), may hold values from -6 to 6
- pre_second: bfloat16 [8, 4, 48, 48, 256], P('dp', None, 'ty', 'tz'), may hold values from -6 to 6
- grad_out: bfloat16 [8, 4, 48, 48, 256], P('dp', None, 'ty', 'tz'), may hold values from -6 to 6
- w_first: bfloat16 [256, 27, 256], P('dp'), may hold values from -0.078125 to 0.078125
- w_second: bfloat16 [256, 27, 256], P('dp'), may hold values from -0.078125 to 0.078125
Outputs:
- grad_input: bfloat16 [8, 4, 48, 48, 256], P('dp', None, 'ty', 'tz')
- grad_w_first: float32 [256, 27, 256], P('dp')
- grad_w_second: float32 [256, 27, 256], P('dp')
All inputs are finite; a program needn't handle non-finite values.
Results may differ from a plain program's by a relative error of at most 0.0049.
Values may be sent and summed in bfloat16 or wider, within the bound.
A program may use at most 128 MiB of HBM per device.

v0:
```python
import math

import jax
import jax.numpy as jnp
from jax import lax
from jax.sharding import PartitionSpec as P


def extended(block, sides, width):
    for axis, dim in sides:
        count = lax.axis_size(axis)
        forward = [(i, i + 1) for i in range(count - 1)]
        backward = [(target, source) for source, target in forward]
        low = lax.ppermute(
            lax.slice_in_dim(block, block.shape[dim] - width, None, axis=dim), axis, forward
        )
        high = lax.ppermute(lax.slice_in_dim(block, 0, width, axis=dim), axis, backward)
        block = jnp.concatenate([low, block, high], axis=dim)
    return block


def data_grad(grad_pad, weight):
    ch_in, _, ch_out = weight.shape
    kernel = weight.reshape(ch_in, 3, 3, 3, ch_out)[:, ::-1, ::-1, ::-1, :]
    return lax.conv_general_dilated(
        grad_pad,
        kernel,
        (1, 1, 1),
        ((1, 1), (0, 0), (0, 0)),
        dimension_numbers=("NDHWC", "ODHWI", "NDHWC"),
        preferred_element_type=jnp.float32,
    )


def filter_grad(act_pad, grad):
    return lax.conv_general_dilated(
        act_pad,
        grad,
        (1, 1, 1),
        ((1, 1), (0, 0), (0, 0)),
        dimension_numbers=("CDHWN", "IDHWO", "NDHWC"),
        preferred_element_type=jnp.float32,
    ).reshape(act_pad.shape[4], -1, grad.shape[4])


def reduce_terms(partial_value):
    ch_in, tap_count, ch_out = partial_value.shape
    dp = lax.axis_size("dp")
    tile = lax.axis_size("ty") * lax.axis_size("tz")
    part = partial_value.astype(jnp.bfloat16).reshape(dp, tile, -1, ch_out)
    part = lax.psum_scatter(part, ("ty", "tz"), scatter_dimension=1, tiled=True)
    share = lax.psum_scatter(part, "dp", scatter_dimension=0, tiled=True)
    share = share.reshape(-1, ch_out)
    whole = lax.all_gather(share, ("ty", "tz"), axis=0, tiled=True)
    return whole.astype(jnp.float32).reshape(-1, tap_count, ch_out)


def local(inputs, pre_first, pre_second, grad_out, w_first, w_second):
    shape = grad_out.shape
    count = (
        shape[0]
        * shape[1]
        * shape[2]
        * shape[3]
        * lax.axis_size("dp")
        * lax.axis_size("ty")
        * lax.axis_size("tz")
    )
    scale = 1.0 / math.sqrt(count)
    sides = (("ty", 2), ("tz", 3))
    zero_half = jnp.zeros((), jnp.bfloat16)
    grad_top = jnp.where(pre_second > 0, grad_out, zero_half)
    active = jnp.where(pre_first > 0, pre_first, zero_half)
    whole_second = lax.all_gather(w_second, "dp", axis=0, tiled=True)
    whole_first = lax.all_gather(w_first, "dp", axis=0, tiled=True)
    part_second = filter_grad(extended(active, sides, 1), grad_top)
    grad_w_second = reduce_terms(part_second * scale)
    upstream = data_grad(extended(grad_top, sides, 1), whole_second)
    grad_low = jnp.where(pre_first > 0, upstream, jnp.zeros((), jnp.float32)).astype(jnp.bfloat16)
    part_first = filter_grad(extended(inputs, sides, 1), grad_low)
    grad_w_first = reduce_terms(part_first * scale)
    grad_input = data_grad(extended(grad_low, sides, 1), whole_first).astype(jnp.bfloat16)
    return (grad_input, grad_w_first, grad_w_second)


def solution(mesh):
    placed = (
        P("dp", None, "ty", "tz", None),
        P("dp", None, "ty", "tz", None),
        P("dp", None, "ty", "tz", None),
        P("dp", None, "ty", "tz", None),
        P("dp", None, None),
        P("dp", None, None),
    )
    return jax.shard_map(
        local,
        mesh=mesh,
        in_specs=placed,
        out_specs=(P("dp", None, "ty", "tz", None), P("dp", None, None), P("dp", None, None)),
        check_vma=False,
    )
```

profile of v0, /device:TPU:0, one launch (start us, length us, event | category | flops | bytes accessed | tf_op | source)
XLA Modules:
  0.0 589.2 jit_solution(10139012923263610299)
XLA Ops:
  8.0 5.4 compare_select_fusion.2
  13.5 1.3 collective-permute-start.1
  14.8 3.0 collective-permute-start
  18.0 1.3 collective-permute-start.8
  19.4 1.3 collective-permute-start.9
  21.0 1.3 collective-permute-start.3
  22.3 5.1 collective-permute-start.2
  27.6 2.1 constant_dynamic-update-slice_fusion.1
  30.4 7.8 %pad_maximum_fusion = bf16[1,4,26,26,256]{4,0,3,2,1:T(2,128)(2,1)S(1)} fusion(bf16[1,4,26,1,256]{4,0,3,2,1:T(2,128)(2,1)S(1)} %collective-permute-done.3, bf16[1,4,1,24,256]{4,0,3,2,1:T(2,128)(2,1)S(1)} %collective-permute-done.1, bf16[1,4,24,24,256]{4,0,3,2,1:T(2,128)(2,1)S(1)} %compare_select_fusion.2, ...), kind=kLoop, calls=%fused_computation.9 | loop fusion | flops 2768896 | bytes 2768896 | tf_op jit(solution)/shard_map/concatenate | solution.py:18
  40.6 37.5 %all-gather.5.cloned.1.call-done = bf16[256,27,256]{2,0,1:T(8,128)(2,1)} async-done(((bf16[32,27,256]{2,0,1:T(8,128)(2,1)}), bf16[256,27,256]{2,0,1:T(8,128)(2,1)}) %all-gather.5.cloned.1.call-update) | async-done | bytes 3538960 | tf_op jit(solution)/shard_map/all_gather | solution.py:74
  78.1 13.6 %fusion.27 = bf16[4,24,8,4,256]{4,2,3,1,0:T(8,128)(2,1)S(1)} fusion(bf16[256,3,3,3,256]{4,0,3,2,1:T(8,128)(2,1)} %bitcast.48, bf16[4,26,1,7,2,256]{5,3,4,1,0,2:T(8,128)(2,1)S(1)} %slice.70, bf16[4,26,1,8,4,256]{5,3,4,1,0,2:T(8,128)(2,1)S(1)} %copy.42, pred[8,4]{0,1:T(4,128)(4,1)S(1)} %copy-done.13), kind=kOutput, calls=%fused_computation.37 | convolution fusion | flops 9068150784 | bytes 7561248 | tf_op jit(solution)/shard_map/conv_general_dilated | solution.py:25
  91.7 0.9 copy.43
  93.0 4.9 compare_select_fusion
  98.1 1.3 collective-permute-start.13
  99.4 3.0 collective-permute-start.12
  102.5 1.2 fusion.42
  103.6 1.3 collective-permute-start.11
  104.9 4.6 collective-permute-start.10
  109.6 1.0 pad_maximum_fusion.8
  110.6 1.3 collective-permute-start.15
  111.9 5.8 collective-permute-start.14
  117.7 54.9 %multiply_convert_fusion.1 = bf16[256,3,3,3,256]{4,0,3,2,1:T(8,128)(2,1)S(1)} fusion(bf16[1,4,24,24,256]{4,0,3,2,1:T(2,128)(2,1)S(1)} %get-tuple-element.26, bf16[1,4,26,1,256]{4,0,3,2,1:T(2,128)(2,1)S(1)} %collective-permute-done.11, bf16[1,4,26,24,256]{4,0,3,2,1:T(2,128)(2,1)} %copy-done.11, bf16[1,4,26,1,256]{4,0,3,2,1:T(2,128)(2,1)S(1)} %collective-permute-done.10), kind=kOutput, calls=%fused_computation.4 | convolution fusion | flops 6802464768 | bytes 6103040 | tf_op jit(solution)/shard_map/conv_general_dilated | solution.py:36
  172.6 5.2 copy.52
  177.7 9.7 %convert_element_type.25 = bf16[8,4,216,256]{3,2,1,0:T(8,128)(2,1)} reshape(bf16[256,3,3,3,256]{4,3,2,1,0:T(4,128)(2,1)} %copy.52) | data formatting | bytes 7077888 | tf_op jit(solution)/shard_map/convert_element_type | solution.py:50
  187.4 41.2 %multiply_convert_fusion = bf16[256,3,3,3,256]{4,0,3,2,1:T(8,128)(2,1)S(1)} fusion(bf16[1,4,24,24,256]{4,0,3,2,1:T(2,128)(2,1)S(1)} %copy-done.3, bf16[1,4,26,1,256]{4,0,3,2,1:T(2,128)(2,1)} %collective-permute-done.15, bf16[1,4,1,24,256]{4,0,3,2,1:T(2,128)(2,1)S(1)} %copy-done.8, bf16[1,4,24,24,256]{4,0,3,2,1:T(2,128)(2,1)} %copy-done.4, ...), kind=kOutput, calls=%fused_computation.3 | convolution fusion | flops 6805233664 | bytes 6103040 | tf_op jit(solution)/shard_map/conv_general_dilated | solution.py:36
  228.6 5.3 copy.54
  233.9 9.5 %convert_element_type.27 = bf16[8,4,216,256]{3,2,1,0:T(8,128)(2,1)} reshape(bf16[256,3,3,3,256]{4,3,2,1,0:T(4,128)(2,1)} %copy.54) | data formatting | bytes 7077888 | tf_op jit(solution)/shard_map/convert_element_type | solution.py:50
  244.8 128.9 %all-reduce.5.cloned.1.call-done = (bf16[8,4,216,256]{3,2,1,0:T(8,128)(2,1)}, bf16[8,4,216,256]{3,2,1,0:T(8,128)(2,1)}) async-done(((bf16[8,4,216,256]{3,2,1,0:T(8,128)(2,1)}, bf16[8,4,216,256]{3,2,1,0:T(8,128)(2,1)}), (bf16[8,4,216,256]{3,2,1,0:T(8,128)(2,1)}, bf16[8,4,216,256]{3,2,1,0:T(8,128)(2,1)})) %all-reduce.5.cloned.1.call-update) | async-done | bytes 7077904
  373.7 2.8 constant_dynamic-slice_fusion.1
  376.8 1.3 collective-permute-start.5
  378.1 3.0 collective-permute-start.4
  381.2 0.9 collective-permute-done.4
  382.4 1.3 collective-permute-start.7
  383.7 4.6 collective-permute-start.6
  388.3 1.3 collective-permute-done.7
  389.5 1.2 collective-permute-done.6
  390.7 7.8 %pad_maximum_fusion.1 = bf16[1,4,26,26,256]{4,0,3,2,1:T(2,128)(2,1)S(1)} fusion(bf16[1,4,26,1,256]{4,0,3,2,1:T(2,128)(2,1)S(1)} %collective-permute-done.7, bf16[1,4,1,24,256]{4,0,3,2,1:T(2,128)(2,1)S(1)} %collective-permute-done.5, bf16[1,4,24,24,256]{4,0,3,2,1:T(2,128)(2,1)S(1)} %copy-done.1, bf16[1,4,1,24,256]{4,0,3,2,1:T(2,128)(2,1)S(1)} %collective-permute-done.4, ...), kind=kLoop, calls=%fused_computation.10 | loop fusion | flops 2768896 | bytes 2768896 | tf_op jit(solution)/shard_map/concatenate | solution.py:18
  400.9 2.8 constant_dynamic-slice_fusion
  403.7 37.6 %all-gather.7.cloned.1.call-done = bf16[256,27,256]{2,0,1:T(8,128)(2,1)} async-done(((bf16[32,27,256]{2,0,1:T(8,128)(2,1)}), bf16[256,27,256]{2,0,1:T(8,128)(2,1)}) %all-gather.7.cloned.1.call-update) | async-done | bytes 3538960 | tf_op jit(solution)/shard_map/all_gather | solution.py:75
  441.4 13.6 %select_convert_fusion = bf16[4,24,8,4,256]{4,2,3,1,0:T(8,128)(2,1)S(1)} fusion(pred[8,4]{0,1:T(4,128)(4,1)S(1)} %copy-done.14, bf16[256,3,3,3,256]{4,0,3,2,1:T(8,128)(2,1)} %bitcast.47, bf16[4,26,1,7,2,256]{5,3,4,1,0,2:T(8,128)(2,1)S(1)} %slice.74, bf16[4,26,1,8,4,256]{5,3,4,1,0,2:T(8,128)(2,1)S(1)} %copy.47), kind=kOutput, calls=%fused_computation.8 | convolution fusion | flops 9068937216 | bytes 7561248 | tf_op jit(solution)/shard_map/conv_general_dilated | solution.py:25
  454.9 0.9 copy.48
  455.9 1.2 copy.55
  457.2 47.7 %reduce-scatter.5.cloned.1.call-done = bf16[1,1,216,256]{3,2,1,0:T(8,128)(2,1)} async-done(((bf16[8,1,216,256]{3,2,1,0:T(8,128)(2,1)}), bf16[1,1,216,256]{3,2,1,0:T(8,128)(2,1)}) %reduce-scatter.5.cloned.1.call-update) | async-done | bytes 110608 | tf_op jit(solution)/shard_map/reduce_scatter | solution.py:52
  504.9 12.4 %all-gather = bf16[1,1,864,256]{3,2,1,0:T(8,128)(2,1)S(1)} all-gather(bf16[1,1,216,256]{3,2,1,0:T(8,128)(2,1)} %reduce-scatter.5.cloned.1.call-done), channel_id=2, replica_groups=mesh['dp'=8,'ty'=2,'tz'=2] {'ty','tz'}, dimensions={2}, use_global_device_ids=true | all-gather | bytes 552960 | tf_op jit(solution)/shard_map/all_gather | solution.py:54
  517.4 1.4 copy.56
  518.9 49.4 %reduce-scatter.7.cloned.1.call-done = bf16[1,1,216,256]{3,2,1,0:T(8,128)(2,1)} async-done(((bf16[8,1,216,256]{3,2,1,0:T(8,128)(2,1)}), bf16[1,1,216,256]{3,2,1,0:T(8,128)(2,1)}) %reduce-scatter.7.cloned.1.call-update) | async-done | bytes 110608 | tf_op jit(solution)/shard_map/reduce_scatter | solution.py:52
  568.3 12.4 %all-gather.1 = bf16[1,1,864,256]{3,2,1,0:T(8,128)(2,1)S(1)} all-gather(bf16[1,1,216,256]{3,2,1,0:T(8,128)(2,1)} %reduce-scatter.7.cloned.1.call-done), channel_id=3, replica_groups=mesh['dp'=8,'ty'=2,'tz'=2] {'ty','tz'}, dimensions={2}, use_global_device_ids=true | all-gather | bytes 552960 | tf_op jit(solution)/shard_map/all_gather | solution.py:54
  580.8 1.4 copy.57
  (76 shorter events, 9.9 us)
Async XLA Ops:
  7.2 70.9 %all-gather.5.cloned.1.call-start = ((), (), s32[]{:S(2)}) async-start(), calls=%async_computation.2 | async-start | bytes 3981312 | tf_op jit(solution)/shard_map/all_gather | solution.py:74
  7.9 10.0 %copy-start.5 = (bf16[1,4,24,24,256]{4,3,2,1,0:T(8,128)(2,1)S(1)}, bf16[1,4,24,24,256]{4,3,2,1,0:T(8,128)(2,1)}, u32[]{:S(2)}) copy-start(bf16[1,4,24,24,256]{4,3,2,1,0:T(8,128)(2,1)} %param.6) | copy-start | bytes 3538948
  7.9 365.8 %all-reduce.5.cloned.1.call-start = ((), (), s32[]{:S(2)}) async-start(), calls=%async_computation.6 | async-start | bytes 14155776
  13.3 17.1 %copy-start.2 = (bf16[1,4,24,24,256]{4,0,3,2,1:T(2,128)(2,1)}, bf16[1,4,24,24,256]{4,0,3,2,1:T(2,128)(2,1)S(1)}, u32[]{:S(2)}) copy-start(bf16[1,4,24,24,256]{4,0,3,2,1:T(2,128)(2,1)S(1)} %compare_select_fusion.2) | copy-start | bytes 3538948
  13.5 7.1 %collective-permute-start.1 = (bf16[1,4,1,24,256]{4,0,3,2,1:T(2,128)(2,1)S(1)}, bf16[1,4,1,24,256]{4,0,3,2,1:T(2,128)(2,1)S(1)}, u32[]{:S(2)}, u32[]{:S(2)}) collective-permute-start(bf16[1,4,1,24,256]{4,0,3,2,1:T(2,128)(2,1)S(1)} %get-tuple-element.24), channel_id=1, source_target_pairs={{2,0},{3,1},{6,4},{7,5},{10,8},{11,9},{14,12},{15,13},{18,16},{19,... | collective-permute-start | bytes 147464 | tf_op jit(solution)/shard_map/ppermute | solution.py:17
  14.8 5.9 collective-permute-start
  18.0 9.5 %collective-permute-start.8 = (bf16[1,4,1,24,256]{4,0,3,2,1:T(2,128)(2,1)S(1)}, bf16[1,4,1,24,256]{4,0,3,2,1:T(2,128)(2,1)S(1)}, u32[]{:S(2)}, u32[]{:S(2)}) collective-permute-start(bf16[1,4,1,24,256]{4,0,3,2,1:T(2,128)(2,1)S(1)} %copy.73), channel_id=1, source_target_pairs={{0,2},{1,3},{4,6},{5,7},{8,10},{9,11},{12,14},{13,15},{16,18},{17,... | collective-permute-start | bytes 147464 | tf_op jit(solution)/shard_map/ppermute | solution.py:14
  19.4 10.3 %collective-permute-start.9 = (bf16[1,4,1,24,256]{4,0,3,2,1:T(2,128)(2,1)S(1)}, bf16[1,4,1,24,256]{4,0,3,2,1:T(2,128)(2,1)S(1)}, u32[]{:S(2)}, u32[]{:S(2)}) collective-permute-start(bf16[1,4,1,24,256]{4,0,3,2,1:T(2,128)(2,1)S(1)} %copy.74), channel_id=1, source_target_pairs={{2,0},{3,1},{6,4},{7,5},{10,8},{11,9},{14,12},{15,13},{18,16},{19,... | collective-permute-start | bytes 147464 | tf_op jit(solution)/shard_map/ppermute | solution.py:17
  21.0 8.8 %collective-permute-start.3 = (bf16[1,4,26,1,256]{4,0,3,2,1:T(2,128)(2,1)S(1)}, bf16[1,4,26,1,256]{4,0,3,2,1:T(2,128)(2,1)S(1)}, u32[]{:S(2)}, u32[]{:S(2)}) collective-permute-start(bf16[1,4,26,1,256]{4,0,3,2,1:T(2,128)(2,1)S(1)} %get-tuple-element.18), channel_id=1, source_target_pairs={{1,0},{3,2},{5,4},{7,6},{9,8},{11,10},{13,12},{15,14},{17,16},{19,... | collective-permute-start | bytes 159752 | tf_op jit(solution)/shard_map/ppermute | solution.py:17
  22.3 8.0 %collective-permute-start.2 = (bf16[1,4,26,1,256]{4,0,3,2,1:T(2,128)(2,1)S(1)}, bf16[1,4,26,1,256]{4,0,3,2,1:T(2,128)(2,1)S(1)}, u32[]{:S(2)}, u32[]{:S(2)}) collective-permute-start(bf16[1,4,26,1,256]{4,0,3,2,1:T(2,128)(2,1)S(1)} %get-tuple-element.17), channel_id=1, source_target_pairs={{0,1},{2,3},{4,5},{6,7},{8,9},{10,11},{12,13},{14,15},{16,17},{18,... | collective-permute-start | bytes 159752 | tf_op jit(solution)/shard_map/ppermute | solution.py:14
  29.8 8.4 %copy-start.11 = (bf16[1,4,26,24,256]{4,0,3,2,1:T(2,128)(2,1)}, bf16[1,4,26,24,256]{4,0,3,2,1:T(2,128)(2,1)S(1)}, u32[]{:S(2)}) copy-start(bf16[1,4,26,24,256]{4,0,3,2,1:T(2,128)(2,1)S(1)} %constant_dynamic-update-slice_fusion) | copy-start | bytes 3833860
  39.7 38.4 %copy-start.13 = (pred[8,4]{0,1:T(4,128)(4,1)S(1)}, pred[8,4]{0,1:T(4,128)(4,1)}, u32[]{:S(2)}) copy-start(pred[8,4]{0,1:T(4,128)(4,1)} %constant.19) | copy-start | bytes 100
  91.7 1.3 copy-start.6
  97.9 11.7 %copy-start.4 = (bf16[1,4,24,24,256]{4,0,3,2,1:T(2,128)(2,1)}, bf16[1,4,24,24,256]{4,0,3,2,1:T(2,128)(2,1)S(1)}, u32[]{:S(2)}) copy-start(bf16[1,4,24,24,256]{4,0,3,2,1:T(2,128)(2,1)S(1)} %get-tuple-element.25) | copy-start | bytes 3538948
  97.9 74.7 %copy-start = (bf16[1,4,24,24,256]{4,0,3,2,1:T(2,128)(2,1)}, bf16[1,4,24,24,256]{4,0,3,2,1:T(2,128)(2,1)S(1)}, u32[]{:S(2)}) copy-start(bf16[1,4,24,24,256]{4,0,3,2,1:T(2,128)(2,1)S(1)} %get-tuple-element.26) | copy-start | bytes 3538948
  98.1 11.4 %collective-permute-start.13 = (bf16[1,4,1,24,256]{4,0,3,2,1:T(2,128)(2,1)S(1)}, bf16[1,4,1,24,256]{4,0,3,2,1:T(2,128)(2,1)S(1)}, u32[]{:S(2)}, u32[]{:S(2)}) collective-permute-start(bf16[1,4,1,24,256]{4,0,3,2,1:T(2,128)(2,1)S(1)} %get-tuple-element.20), channel_id=1, source_target_pairs={{2,0},{3,1},{6,4},{7,5},{10,8},{11,9},{14,12},{15,13},{18,16},{19,... | collective-permute-start | bytes 147464 | tf_op jit(solution)/shard_map/ppermute | solution.py:17
  99.4 10.1 %collective-permute-start.12 = (bf16[1,4,1,24,256]{4,0,3,2,1:T(2,128)(2,1)S(1)}, bf16[1,4,1,24,256]{4,0,3,2,1:T(2,128)(2,1)S(1)}, u32[]{:S(2)}, u32[]{:S(2)}) collective-permute-start(bf16[1,4,1,24,256]{4,0,3,2,1:T(2,128)(2,1)S(1)} %get-tuple-element.19), channel_id=1, source_target_pairs={{0,2},{1,3},{4,6},{5,7},{8,10},{9,11},{12,14},{13,15},{16,18},{17,... | collective-permute-start | bytes 147464 | tf_op jit(solution)/shard_map/ppermute | solution.py:14
  103.6 14.0 %collective-permute-start.11 = (bf16[1,4,26,1,256]{4,0,3,2,1:T(2,128)(2,1)S(1)}, bf16[1,4,26,1,256]{4,0,3,2,1:T(2,128)(2,1)S(1)}, u32[]{:S(2)}, u32[]{:S(2)}) collective-permute-start(bf16[1,4,26,1,256]{4,0,3,2,1:T(2,128)(2,1)S(1)} %get-tuple-element.14), channel_id=1, source_target_pairs={{1,0},{3,2},{5,4},{7,6},{9,8},{11,10},{13,12},{15,14},{17,16},{19,... | collective-permute-start | bytes 159752 | tf_op jit(solution)/shard_map/ppermute | solution.py:17
  104.9 12.7 %collective-permute-start.10 = (bf16[1,4,26,1,256]{4,0,3,2,1:T(2,128)(2,1)S(1)}, bf16[1,4,26,1,256]{4,0,3,2,1:T(2,128)(2,1)S(1)}, u32[]{:S(2)}, u32[]{:S(2)}) collective-permute-start(bf16[1,4,26,1,256]{4,0,3,2,1:T(2,128)(2,1)S(1)} %get-tuple-element.13), channel_id=1, source_target_pairs={{0,1},{2,3},{4,5},{6,7},{8,9},{10,11},{12,13},{14,15},{16,17},{18,... | collective-permute-start | bytes 159752 | tf_op jit(solution)/shard_map/ppermute | solution.py:14
  109.5 8.2 %copy-start.7 = (bf16[1,4,1,24,256]{4,0,3,2,1:T(2,128)(2,1)}, bf16[1,4,1,24,256]{4,0,3,2,1:T(2,128)(2,1)S(1)}, u32[]{:S(2)}) copy-start(bf16[1,4,1,24,256]{4,0,3,2,1:T(2,128)(2,1)S(1)} %collective-permute-done.13) | copy-start | bytes 147460
  109.5 8.1 %copy-start.9 = (bf16[1,4,1,24,256]{4,0,3,2,1:T(2,128)(2,1)}, bf16[1,4,1,24,256]{4,0,3,2,1:T(2,128)(2,1)S(1)}, u32[]{:S(2)}) copy-start(bf16[1,4,1,24,256]{4,0,3,2,1:T(2,128)(2,1)S(1)} %collective-permute-done.12) | copy-start | bytes 147460
  110.6 76.8 %collective-permute-start.15 = (bf16[1,4,26,1,256]{4,0,3,2,1:T(2,128)(2,1)}, bf16[1,4,26,1,256]{4,0,3,2,1:T(2,128)(2,1)}, u32[]{:S(2)}, u32[]{:S(2)}) collective-permute-start(bf16[1,4,26,1,256]{4,0,3,2,1:T(2,128)(2,1)} %get-tuple-element.12), channel_id=1, source_target_pairs={{1,0},{3,2},{5,4},{7,6},{9,8},{11,10},{13,12},{15,14},{17,16},{19,... | collective-permute-start | bytes 159752 | tf_op jit(solution)/shard_map/ppermute | solution.py:17
  111.9 75.5 %collective-permute-start.14 = (bf16[1,4,26,1,256]{4,0,3,2,1:T(2,128)(2,1)}, bf16[1,4,26,1,256]{4,0,3,2,1:T(2,128)(2,1)}, u32[]{:S(2)}, u32[]{:S(2)}) collective-permute-start(bf16[1,4,26,1,256]{4,0,3,2,1:T(2,128)(2,1)} %get-tuple-element.11), channel_id=1, source_target_pairs={{0,1},{2,3},{4,5},{6,7},{8,9},{10,11},{12,13},{14,15},{16,17},{18,... | collective-permute-start | bytes 159752 | tf_op jit(solution)/shard_map/ppermute | solution.py:14
  177.7 9.7 %copy-start.3 = (bf16[1,4,24,24,256]{4,0,3,2,1:T(2,128)(2,1)S(1)}, bf16[1,4,24,24,256]{4,0,3,2,1:T(2,128)(2,1)}, u32[]{:S(2)}) copy-start(bf16[1,4,24,24,256]{4,0,3,2,1:T(2,128)(2,1)} %copy-done.2) | copy-start | bytes 3538948
  177.7 9.7 %copy-start.8 = (bf16[1,4,1,24,256]{4,0,3,2,1:T(2,128)(2,1)S(1)}, bf16[1,4,1,24,256]{4,0,3,2,1:T(2,128)(2,1)}, u32[]{:S(2)}) copy-start(bf16[1,4,1,24,256]{4,0,3,2,1:T(2,128)(2,1)} %copy-done.7) | copy-start | bytes 147460
  177.7 9.7 %copy-start.10 = (bf16[1,4,1,24,256]{4,0,3,2,1:T(2,128)(2,1)S(1)}, bf16[1,4,1,24,256]{4,0,3,2,1:T(2,128)(2,1)}, u32[]{:S(2)}) copy-start(bf16[1,4,1,24,256]{4,0,3,2,1:T(2,128)(2,1)} %copy-done.9) | copy-start | bytes 147460
  243.4 0.8 copy-start.12
  243.4 133.2 %copy-start.1 = (bf16[1,4,24,24,256]{4,0,3,2,1:T(2,128)(2,1)S(1)}, bf16[1,4,24,24,256]{4,0,3,2,1:T(2,128)(2,1)}, u32[]{:S(2)}) copy-start(bf16[1,4,24,24,256]{4,0,3,2,1:T(2,128)(2,1)} %copy-done) | copy-start | bytes 3538948
  243.4 197.9 %all-gather.7.cloned.1.call-start = ((), (), s32[]{:S(2)}) async-start(), calls=%async_computation.3 | async-start | bytes 3981312 | tf_op jit(solution)/shard_map/all_gather | solution.py:75
  244.2 260.7 %reduce-scatter.5.cloned.1.call-start = ((), (), s32[]{:S(2)}) async-start(), calls=%async_computation.4 | async-start | bytes 995328 | tf_op jit(solution)/shard_map/reduce_scatter | solution.py:52
  376.5 191.7 %reduce-scatter.7.cloned.1.call-start = ((), (), s32[]{:S(2)}) async-start(), calls=%async_computation.5 | async-start | bytes 995328 | tf_op jit(solution)/shard_map/reduce_scatter | solution.py:52
  376.8 4.3 collective-permute-start.5
  378.1 4.0 collective-permute-start.4
  382.4 7.1 %collective-permute-start.7 = (bf16[1,4,26,1,256]{4,0,3,2,1:T(2,128)(2,1)S(1)}, bf16[1,4,26,1,256]{4,0,3,2,1:T(2,128)(2,1)S(1)}, u32[]{:S(2)}, u32[]{:S(2)}) collective-permute-start(bf16[1,4,26,1,256]{4,0,3,2,1:T(2,128)(2,1)S(1)} %get-tuple-element.16), channel_id=1, source_target_pairs={{1,0},{3,2},{5,4},{7,6},{9,8},{11,10},{13,12},{15,14},{17,16},{19,... | collective-permute-start | bytes 159752 | tf_op jit(solution)/shard_map/ppermute | solution.py:17
  383.7 7.0 %collective-permute-start.6 = (bf16[1,4,26,1,256]{4,0,3,2,1:T(2,128)(2,1)S(1)}, bf16[1,4,26,1,256]{4,0,3,2,1:T(2,128)(2,1)S(1)}, u32[]{:S(2)}, u32[]{:S(2)}) collective-permute-start(bf16[1,4,26,1,256]{4,0,3,2,1:T(2,128)(2,1)S(1)} %get-tuple-element.15), channel_id=1, source_target_pairs={{0,1},{2,3},{4,5},{6,7},{8,9},{10,11},{12,13},{14,15},{16,17},{18,... | collective-permute-start | bytes 159752 | tf_op jit(solution)/shard_map/ppermute | solution.py:14
  400.7 40.7 %copy-start.14 = (pred[8,4]{0,1:T(4,128)(4,1)S(1)}, pred[8,4]{0,1:T(4,128)(4,1)}, u32[]{:S(2)}) copy-start(pred[8,4]{0,1:T(4,128)(4,1)} %constant.19) | copy-start | bytes 100
Sparse Core Ops, SparseCore 0:
  10.2 67.8 all-gather.4
  243.5 130.1 all-reduce.4
  375.9 65.4 all-gather.6
  445.2 59.6 reduce-scatter.4
  508.1 60.0 reduce-scatter.6
where the time goes:
time: 594 us; the launch traced here: 589 us
  waiting for transfers between devices  307 us (52%)
  matrix products  123 us (21%)
  local copies, waits for them, and re-layouts  51.4 us (9%)
  starting transfers between devices  41 us (7%)
  other arithmetic  27.5 us (5%)
  blocking collectives  24.8 us (4%)
  between operations  14.7 us (2%)
    unnamed x6, waiting for transfers between devices  130 us
    reduce_scatter x2, waiting for transfers between devices, reduce_terms(): share = lax.psum_scatter(part, 'dp', scatter_dimension=0, tiled=True)  97.1 us
    conv_general_dilated x2, matrix products, filter_grad(): lax.conv_general_dilated(act_pad, grad, (1, 1, 1), ((1, 1), (0, 0), (0, 0...  96.1 us
    all_gather x1, waiting for transfers between devices, local(): whole_first = lax.all_gather(w_first, 'dp', axis=0, tiled=True)  37.6 us
    all_gather x1, waiting for transfers between devices, local(): whole_second = lax.all_gather(w_second, 'dp', axis=0, tiled=True)  37.5 us
    ppermute x8, starting transfers between devices, extended(): lax.ppermute(lax.slice_in_dim(block, block.shape[dim] - width, None, axis...  30.4 us
    convert_element_type x4, local copies, waits for them, and re-layouts, reduce_terms(): part = partial_value.astype(jnp.bfloat16).reshape(dp, tile, -1, ch_out)  29.6 us
    conv_general_dilated x2, matrix products, data_grad(): lax.conv_general_dilated(grad_pad, kernel, (1, 1, 1), ((1, 1), (0, 0), (0...  27.2 us
  transfers between devices with their start and end apart: 21, of which 9 were waited for; matrix products, arithmetic and copies ran while one was open for 21% of the time, Pallas kernels for 0%

commit v1 on v0

v1 whole, which is shorter than its diff:
```python
import functools
import math

import jax
import jax.numpy as jnp
from jax import lax
from jax.experimental import pallas as pl
from jax.experimental.pallas import tpu as pltpu
from jax.sharding import PartitionSpec as P

MESH = pl.DeviceIdType.MESH
VMEM = pl.BlockSpec(memory_space=pltpu.VMEM)
NT = (((1,), (1,)), ((), ()))


def extended(block, sides, width):
    for axis, dim in sides:
        count = lax.axis_size(axis)
        forward = [(i, i + 1) for i in range(count - 1)]
        backward = [(target, source) for source, target in forward]
        low = lax.ppermute(
            lax.slice_in_dim(block, block.shape[dim] - width, None, axis=dim), axis, forward
        )
        high = lax.ppermute(lax.slice_in_dim(block, 0, width, axis=dim), axis, backward)
        block = jnp.concatenate([low, block, high], axis=dim)
    return block


def shifted_views(field, order):
    depth, high, wide, _ = field.shape
    high, wide = high - 2, wide - 2
    lanes = jnp.concatenate([field[:, :, c : c + wide, :] for c in order], axis=-1)
    lanes = jnp.pad(lanes, ((1, 1), (0, 0), (0, 0), (0, 0)))
    if (2 * wide) % 16 == 0:
        return [
            lanes.reshape(depth + 2, (high + 2) * wide, -1),
            lanes[:, 1 : 1 + high].reshape(depth + 2, high * wide, -1),
        ]
    return [lanes[:, b : b + high].reshape(depth + 2, high * wide, -1) for b in range(3)]


def view_at(views, b, pitch):
    if len(views) == 2:
        return (views[1], 0) if b == 1 else (views[0], b * pitch)
    return views[b], 0


def filter_terms(views, pitch, grad_t, out):
    rows = grad_t.shape[1]
    ch = grad_t.shape[0]
    depth = views[0].shape[0] - 2
    plane = rows // depth
    for tap in range(27, out.shape[0]):
        out[tap] = jnp.zeros(out.shape[1:], out.dtype)

    for b in range(3):
        view, start = view_at(views, b, pitch)

        def step(a, _, b=b, view=view, start=start):
            block = view[pl.ds(a, depth), start : start + plane, :].reshape(rows, -1)
            acc = jnp.dot(grad_t[...], block, preferred_element_type=jnp.float32)
            for c in range(3):
                out[9 * a + 3 * b + c] = acc[:, c * ch : (c + 1) * ch].T.astype(out.dtype)
            return 0

        lax.fori_loop(0, 3, step, 0)


def data_plane(views, pitch, weight, acc, x):
    plane, ch = acc.shape
    acc[...] = jnp.zeros_like(acc)

    def step(a, _):
        total = None
        for b in range(3):
            view, start = view_at(views, 2 - b, pitch)
            block = view[x + 2 - a, start : start + plane, :]
            first = pl.multiple_of((9 * a + 3 * b) * ch, 128)
            term = lax.dot_general(
                block,
                weight[:, pl.ds(first, 3 * ch)],
                NT,
                preferred_element_type=jnp.float32,
            )
            total = term if total is None else total + term
        acc[...] += total
        return 0

    lax.fori_loop(0, 3, step, 0)


def enter(sizes):
    barrier = pltpu.get_barrier_semaphore()
    count = 0
    for axis, size in sizes.items():
        me = lax.axis_index(axis)
        for d in range(1, size):
            pl.semaphore_signal(
                barrier, inc=1, device_id={axis: lax.rem(me + d, size)}, device_id_type=MESH
            )
            count += 1
    pl.semaphore_wait(barrier, count)


def fan_out(axis, size, source, target, send, recv):
    me = lax.axis_index(axis)
    copies = []
    for d in range(1, size):
        peer = lax.rem(me + d, size)
        copies.append(
            pltpu.make_async_remote_copy(
                src_ref=source(peer),
                dst_ref=target(d),
                send_sem=send.at[d],
                recv_sem=recv.at[d],
                device_id={axis: peer},
                device_id_type=MESH,
            )
        )
    for copy in copies:
        copy.start()
    return copies


def gather_stages(sizes, shard, whole, sems):
    ndp, nty, ntz = sizes["dp"], sizes["ty"], sizes["tz"]
    dp, ty, tz = lax.axis_index("dp"), lax.axis_index("ty"), lax.axis_index("tz")
    rows, lanes = shard.shape
    part = lanes // (nty * ntz)
    mine = pl.ds(pl.multiple_of((ty * ntz + tz) * part, 128), part)
    group = pl.ds(pl.multiple_of(ty * ntz * part, 128), ntz * part)
    own = pl.ds(pl.multiple_of(dp * rows, 16), rows)

    whole[own, mine] = shard[:, mine]
    copies = fan_out(
        "dp", ndp, lambda peer: shard.at[:, mine], lambda d: whole.at[own, mine], sems.at[0], sems.at[1]
    )
    yield
    for copy in copies:
        copy.wait()
    copies = fan_out(
        "tz", ntz, lambda peer: whole.at[:, mine], lambda d: whole.at[:, mine], sems.at[2], sems.at[3]
    )
    yield
    for copy in copies:
        copy.wait()
    copies = fan_out(
        "ty", nty, lambda peer: whole.at[:, group], lambda d: whole.at[:, group], sems.at[4], sems.at[5]
    )
    yield
    for copy in copies:
        copy.wait()


def reduce_stages(sizes, part, out, bufs, sems):
    ndp, nty, ntz = sizes["dp"], sizes["ty"], sizes["tz"]
    dp, ty, tz = lax.axis_index("dp"), lax.axis_index("ty"), lax.axis_index("tz")
    over_ty, sum_ty, over_tz, sum_tz, over_dp = bufs
    wide, few, rows = sum_ty.shape[0], sum_tz.shape[0], over_dp.shape[2]

    copies = fan_out(
        "ty", nty, lambda peer: part.at[pl.ds(peer * wide, wide)], lambda d: over_ty.at[d - 1],
        sems.at[0], sems.at[1],
    )
    yield
    for copy in copies:
        copy.wait()

    def add_ty(t, _):
        total = part[ty * wide + t].astype(jnp.float32)
        for d in range(nty - 1):
            total += over_ty[d, t].astype(jnp.float32)
        sum_ty[t] = total.astype(sum_ty.dtype)
        return 0

    lax.fori_loop(0, wide, add_ty, 0)
    copies = fan_out(
        "tz", ntz, lambda peer: sum_ty.at[pl.ds(peer * few, few)], lambda d: over_tz.at[d - 1],
        sems.at[2], sems.at[3],
    )
    yield
    for copy in copies:
        copy.wait()

    def add_tz(t, _):
        total = sum_ty[tz * few + t].astype(jnp.float32)
        for d in range(ntz - 1):
            total += over_tz[d, t].astype(jnp.float32)
        sum_tz[t] = total.astype(sum_tz.dtype)
        return 0

    lax.fori_loop(0, few, add_tz, 0)
    copies = fan_out(
        "dp", ndp,
        lambda peer: sum_tz.at[:, pl.ds(pl.multiple_of(peer * rows, 16), rows)],
        lambda d: over_dp.at[d - 1], sems.at[4], sems.at[5],
    )
    yield
    for copy in copies:
        copy.wait()
    first = (ty * ntz + tz) * few

    def add_dp(t, _):
        total = sum_tz[t, pl.ds(pl.multiple_of(dp * rows, 16), rows)].astype(jnp.float32)
        for d in range(ndp - 1):
            total += over_dp[d, t].astype(jnp.float32)
        out[first + t] = total
        return 0

    lax.fori_loop(0, few, add_dp, 0)
    mine = out.at[pl.ds(first, few)]
    copies = fan_out("tz", ntz, lambda peer: mine, lambda d: mine, sems.at[6], sems.at[7])
    yield
    for copy in copies:
        copy.wait()
    group = out.at[pl.ds(ty * wide, wide)]
    copies = fan_out("ty", nty, lambda peer: group, lambda d: group, sems.at[8], sems.at[9])
    yield
    for copy in copies:
        copy.wait()


def advance(stages):
    for stage in stages:
        next(stage, None)


def finish(stages):
    for stage in stages:
        for _ in stage:
            pass


def first_kernel(sizes, pitch, count, *refs):
    views, (grad_t, shard, terms, whole, sems) = refs[:count], refs[count:]
    enter(sizes)
    stages = [gather_stages(sizes, shard, whole, sems)]
    advance(stages)
    filter_terms(views, pitch, grad_t, terms)
    finish(stages)


def terms_kernel(pitch, count, *refs):
    views, (grad_t, terms) = refs[:count], refs[count:]
    filter_terms(views, pitch, grad_t, terms)


def data_kernel(sizes, pitch, count, masked, *refs):
    views, refs = refs[:count], list(refs[count:])
    weight, part = refs[:2]
    del refs[:2]
    if masked:
        pre, shard = refs[:2]
        del refs[:2]
    grad, reduced = refs[:2]
    del refs[:2]
    if masked:
        whole = refs.pop(0)
        gather_sems = refs.pop()
    acc, *bufs, sems = refs
    enter(sizes)
    stages = [reduce_stages(sizes, part, reduced, bufs, sems)]
    if masked:
        stages.append(gather_stages(sizes, shard, whole, gather_sems))
    for x in range(grad.shape[0]):
        advance(stages)
        data_plane(views, pitch, weight, acc, x)
        value = acc[...]
        if masked:
            value = jnp.where(pre[x].astype(jnp.float32) > 0, value, 0.0)
        grad[x] = value.astype(grad.dtype)
    finish(stages)


def local(inputs, pre_first, pre_second, grad_out, w_first, w_second):
    frames, depth, high, wide, ch = grad_out.shape
    sizes = {axis: lax.axis_size(axis) for axis in ("dp", "ty", "tz")}
    ndp, nty, ntz = sizes["dp"], sizes["ty"], sizes["tz"]
    tiles = nty * ntz
    scale = 1.0 / math.sqrt(frames * depth * high * wide * ndp * tiles)
    sides = (("ty", 2), ("tz", 3))
    half = jnp.bfloat16
    rows, plane = depth * high * wide, high * wide
    taps = -(-27 // tiles) * tiles
    few, share = taps // tiles, ch // ndp
    lanes = taps * ch
    shape = jax.ShapeDtypeStruct
    dma = pltpu.SemaphoreType.DMA

    zero_half = jnp.zeros((), half)
    grad_top = jnp.where(pre_second > 0, grad_out, zero_half)
    active = jnp.where(pre_first > 0, pre_first, zero_half)
    padded = extended(jnp.concatenate([active, grad_top, inputs], axis=0), sides, 1)
    forward, backward = (0, 1, 2), (2, 1, 0)
    act_views = shifted_views(padded[0], forward)
    top_views = shifted_views(padded[1], backward)
    in_views = shifted_views(padded[2], forward)
    count = len(act_views)
    shards = [
        jnp.pad(w.reshape(share, -1), ((0, 0), (0, lanes - 27 * ch))) for w in (w_second, w_first)
    ]
    whole_shape = shape((ch, lanes), half)
    terms_shape = shape((taps, ch, ch), half)

    def specs(n):
        return [VMEM] * n

    def run(body, out_shape, scratch, name, operands, collective_id=None):
        params = dict(vmem_limit_bytes=56 * 1024 * 1024)
        if collective_id is not None:
            params.update(collective_id=collective_id, has_side_effects=True)
        return pl.pallas_call(
            body,
            out_shape=out_shape,
            in_specs=specs(len(operands)),
            out_specs=jax.tree.map(lambda _: VMEM, out_shape),
            scratch_shapes=scratch,
            compiler_params=pltpu.CompilerParams(**params),
            name=name,
        )(*operands)

    most = max(sizes.values())
    terms_second, whole_second = run(
        functools.partial(first_kernel, sizes, wide, count),
        (terms_shape, whole_shape),
        [dma((6, most))],
        "terms_second",
        (*act_views, grad_top.reshape(rows, ch).T, shards[0]),
        0,
    )
    reduce_scratch = [
        pltpu.VMEM((plane, ch), jnp.float32),
        pltpu.VMEM((nty - 1, ntz * few, ch, ch), half),
        pltpu.VMEM((ntz * few, ch, ch), half),
        pltpu.VMEM((ntz - 1, few, ch, ch), half),
        pltpu.VMEM((few, ch, ch), half),
        pltpu.VMEM((ndp - 1, few, share, ch), half),
        dma((10, most)),
    ]
    grad_shape = shape((depth, plane, ch), half)
    reduced_shape = shape((taps, share, ch), jnp.float32)
    grad_low, reduced_second, whole_first = run(
        functools.partial(data_kernel, sizes, wide, count, True),
        (grad_shape, reduced_shape, whole_shape),
        [*reduce_scratch, dma((6, most))],
        "grad_low",
        (*top_views, whole_second, terms_second, pre_first.reshape(depth, plane, ch), shards[1]),
        1,
    )
    terms_first = run(
        functools.partial(terms_kernel, wide, count),
        terms_shape,
        [],
        "terms_first",
        (*in_views, grad_low.reshape(rows, ch).T),
    )
    low_views = shifted_views(
        extended(grad_low.reshape(1, depth, high, wide, ch), sides, 1)[0], backward
    )
    grad_input, reduced_first = run(
        functools.partial(data_kernel, sizes, wide, count, False),
        (grad_shape, reduced_shape),
        reduce_scratch,
        "grad_input",
        (*low_views, whole_first, terms_first),
        2,
    )

    def filter_out(reduced):
        return reduced[:27].transpose(1, 0, 2) * scale

    return (
        grad_input.reshape(grad_out.shape),
        filter_out(reduced_first),
        filter_out(reduced_second),
    )


def solution(mesh):
    placed = (
        P("dp", None, "ty", "tz", None),
        P("dp", None, "ty", "tz", None),
        P("dp", None, "ty", "tz", None),
        P("dp", None, "ty", "tz", None),
        P("dp", None, None),
        P("dp", None, None),
    )
    return jax.shard_map(
        local,
        mesh=mesh,
        in_specs=placed,
        out_specs=(P("dp", None, "ty", "tz", None), P("dp", None, None), P("dp", None, None)),
        check_vma=False,
    )
```

time: 594 us -> 280 us (0.47)
  waiting for transfers between devices: 307 us -> 2.6 us
  Pallas kernels: 0 us -> 204 us
  matrix products: 123 us -> 0 us
  blocking collectives: 24.8 us -> 0 us
  local copies, waits for them, and re-layouts: 51.4 us -> 30.6 us
  starting transfers between devices: 41 us -> 22.2 us
  between operations: 14.7 us -> 0.92 us
  other arithmetic: 27.5 us -> 14.8 us
    pallas_call x0 -> x4, Pallas kernels: none -> 204 us  [run(): pl.pallas_call(body, out_shape=out_shape, in_specs=specs(len(operands)),...]
    unnamed x6 -> x0, waiting for transfers between devices: 130 us -> none
    conv_general_dilated x4 -> x0, matrix products: 123 us -> none  [the longest x2 96.1 us: filter_grad(): lax.conv_general_dilated(act_pad, grad, (1, 1, 1), ((1, 1), (0, 0), (0, 0...]
    reduce_scatter x2 -> x0, waiting for transfers between devices: 97.1 us -> none  [reduce_terms(): share = lax.psum_scatter(part, 'dp', scatter_dimension=0, tiled=True)]
    all_gather x2 -> x0, waiting for transfers between devices: 75.1 us -> none  [the longest x1 37.6 us: local(): whole_first = lax.all_gather(w_first, 'dp', axis=0, tiled=True)]
    convert_element_type x6 -> x0, local copies, waits for them, and re-layouts: 30.6 us -> none  [the longest x4 29.6 us: reduce_terms(): part = partial_value.astype(jnp.bfloat16).reshape(dp, tile, -1, ch_out)]
    all_gather x2 -> x0, blocking collectives: 24.8 us -> none  [reduce_terms(): whole = lax.all_gather(share, ('ty', 'tz'), axis=0, tiled=True)]
    slice x1 -> x8, local copies, waits for them, and re-layouts: 0.01 us -> 15.4 us  [the longest x4 11.6 us: shifted_views(): lanes[:, 1:1 + high].reshape(depth + 2, high * wide, -1)]
  transfers between devices with their start and end apart: 21 -> 8, of which waited for: 9 -> 2; matrix products, arithmetic and copies ran while one was open for 21% -> 4% of each run, Pallas kernels for 0% -> 6%
where the time goes in v1:
time: 280 us; the launch traced here: 276 us
  Pallas kernels  204 us (73%)
  local copies, waits for them, and re-layouts  30.6 us (11%)
  starting transfers between devices  22.2 us (8%)
  other arithmetic  14.8 us (5%)
    pallas_call x4, Pallas kernels, run(): pl.pallas_call(body, out_shape=out_shape, in_specs=specs(len(operands)),...  204 us
    ppermute x4, starting transfers between devices, extended(): lax.ppermute(lax.slice_in_dim(block, block.shape[dim] - width, None, axis...  17.1 us
    slice x4, local copies, waits for them, and re-layouts, shifted_views(): lanes[:, 1:1 + high].reshape(depth + 2, high * wide, -1)  11.6 us
    unnamed x23, local copies, waits for them, and re-layouts  6.93 us
  transfers between devices with their start and end apart: 8, of which 2 were waited for; matrix products, arithmetic and copies ran while one was open for 4% of the time, Pallas kernels for 6%

profile of v1, /device:TPU:0, one launch (start us, length us, event | category | flops | bytes accessed | tf_op | source)
XLA Modules:
  0.0 275.6 jit_solution(17542560645065232311)
XLA Ops:
  0.6 2.3 compare_select_fusion
  2.9 0.0 copy-done.5
  3.0 1.3 collective-permute-start.1
  4.3 3.0 %collective-permute-start = (bf16[3,4,1,24,256]{4,3,2,1,0:T(8,128)(2,1)S(1)}, bf16[3,4,1,24,256]{4,3,2,1,0:T(8,128)(2,1)S(1)}, u32[]{:S(2)}, u32[]{:S(2)}) collective-permute-start(bf16[3,4,1,24,256]{4,3,2,1,0:T(8,128)(2,1)S(1)} %get-tuple-element.22), channel_id=1, source_target_pairs={{0,2},{1,3},{4,6},{5,7},{8,10},{9,11},{12,14},{13,15},{16,18},{17,... | collective-permute-start | bytes 442376 | tf_op jit(solution)/shard_map/ppermute | solution.py:21
  7.4 0.0 collective-permute-done.1
  7.4 1.0 collective-permute-done
  8.3 1.4 pad_maximum_fusion.5
  9.8 1.3 collective-permute-start.3
  11.1 6.3 %collective-permute-start.2 = (bf16[3,4,26,1,256]{4,3,2,1,0:T(2,128)(2,1)}, bf16[3,4,26,1,256]{4,3,2,1,0:T(2,128)(2,1)}, u32[]{:S(2)}, u32[]{:S(2)}) collective-permute-start(bf16[3,4,26,1,256]{4,3,2,1,0:T(2,128)(2,1)} %get-tuple-element.20), channel_id=1, source_target_pairs={{0,1},{2,3},{4,5},{6,7},{8,9},{10,11},{12,13},{14,15},{16,17},{18,... | collective-permute-start | bytes 479240 | tf_op jit(solution)/shard_map/ppermute | solution.py:21
  17.4 1.5 copy.13
  18.9 1.1 copy.17
  20.0 1.0 copy.18
  21.0 0.8 pad.22.refs_3_
  21.8 0.8 pad.23.refs_5_
  22.6 1.6 collective-permute-done.2
  24.3 4.8 %pad_maximum_fusion = bf16[3,4,26,26,256]{4,3,2,1,0:T(8,128)(2,1)S(1)} fusion(bf16[3,4,26,1,256]{4,3,2,1,0:T(2,128)(2,1)} %collective-permute-done.3, bf16[3,4,1,24,256]{4,3,2,1,0:T(8,128)(2,1)S(1)} %copy-done.8, bf16[1,4,24,24,256]{4,3,2,1,0:T(8,128)(2,1)S(1)} %copy-done.5, bf16[1,4,24,24,256]{4,3,2,1,0:T(8,128)(2,1)S(1)} %get-tuple-element.41, ...), kind=kLoop, calls=%fused_computation.17 | loop fusion | flops 29073408 | bytes 8306688 | tf_op jit(solution)/shard_map/concatenate | solution.py:25
  29.0 0.7 slice_bitcast_fusion
  29.7 0.9 fusion.14
  30.6 0.4 fusion.8
  31.1 2.9 %slice.120 = bf16[6,24,24,768]{3,2,1,0:T(8,128)(2,1)} slice(bf16[6,26,24,768]{3,2,1,0:T(8,128)(2,1)S(1)} %fusion.8), slice={[0:6], [1:25], [0:24], [0:768]} | slice | bytes 10616832 | tf_op jit(solution)/shard_map/slice | solution.py:37
  34.0 1.2 copy-done
  35.2 1.0 fusion.13
  36.2 0.4 fusion.10
  36.6 2.9 %slice.125 = bf16[6,24,24,768]{3,2,1,0:T(8,128)(2,1)} slice(bf16[6,26,24,768]{3,2,1,0:T(8,128)(2,1)S(1)} %fusion.10), slice={[0:6], [1:25], [0:24], [0:768]} | slice | bytes 10616832 | tf_op jit(solution)/shard_map/slice | solution.py:37
  39.5 1.3 copy-done.3
  40.8 52.5 %terms_second.1 = (bf16[28,256,256]{2,1,0:T(8,128)(2,1)}, bf16[256,7168]{1,0:T(8,128)(2,1)}) custom-call(bf16[6,624,768]{2,1,0:T(8,128)(2,1)} %bitcast.34, bf16[6,576,768]{2,1,0:T(8,128)(2,1)} %bitcast.39, bf16[256,2304]{1,0:T(8,128)(2,1)} %bitcast.44, bf16[32,7168]{1,0:T(8,128)(2,1)} %pad.22.refs_3_), custom_call_target="tpu_custom_call" | custom-call | tf_op jit(solution)/shard_map/terms_second/pallas_call | solution.py:312
  93.3 75.5 %grad_low.1 = (bf16[4,576,256]{2,1,0:T(8,128)(2,1)}, f32[28,32,256]{2,1,0:T(8,128)}, bf16[256,7168]{1,0:T(8,128)(2,1)}) custom-call(bf16[6,624,768]{2,1,0:T(8,128)(2,1)} %bitcast.31, bf16[6,576,768]{2,1,0:T(8,128)(2,1)} %bitcast.37, bf16[256,7168]{1,0:T(8,128)(2,1)} %get-tuple-element.10.refs_2_, bf16[28,256,256]{2,1,0:T(8,128)(2,1)} %get-tuple-element.11.refs_3_, ...), custom_call_target="tpu_custom_call" | custom-call | tf_op jit(solution)/shard_map/grad_low/pallas_call | solution.py:312
  168.8 0.8 fusion.15
  169.6 1.3 collective-permute-start.5
  170.9 3.2 %collective-permute-start.4 = (bf16[1,4,1,24,256]{4,3,2,1,0:T(8,128)(2,1)S(1)}, bf16[1,4,1,24,256]{4,3,2,1,0:T(8,128)(2,1)S(1)}, u32[]{:S(2)}, u32[]{:S(2)}) collective-permute-start(bf16[1,4,1,24,256]{4,3,2,1,0:T(8,128)(2,1)S(1)} %get-tuple-element.38), channel_id=1, source_target_pairs={{0,2},{1,3},{4,6},{5,7},{8,10},{9,11},{12,14},{13,15},{16,18},{17,... | collective-permute-start | bytes 147464 | tf_op jit(solution)/shard_map/ppermute | solution.py:21
  174.1 0.9 fusion.11
  175.0 0.4 select_maximum_fusion
  175.5 0.8 copy-done.4
  176.3 0.2 pad_maximum_fusion.11
  176.4 1.3 collective-permute-start.7
  177.7 4.6 %collective-permute-start.6 = (bf16[1,4,26,1,256]{4,3,2,1,0:T(2,128)(2,1)S(1)}, bf16[1,4,26,1,256]{4,3,2,1,0:T(2,128)(2,1)S(1)}, u32[]{:S(2)}, u32[]{:S(2)}) collective-permute-start(bf16[1,4,26,1,256]{4,3,2,1,0:T(2,128)(2,1)S(1)} %get-tuple-element.36), channel_id=1, source_target_pairs={{0,1},{2,3},{4,5},{6,7},{8,9},{10,11},{12,13},{14,15},{16,17},{18,... | collective-permute-start | bytes 159752 | tf_op jit(solution)/shard_map/ppermute | solution.py:21
  182.3 1.0 multiply_bitcast_fusion
  183.3 2.8 %slice.136 = bf16[6,24,24,768]{3,2,1,0:T(8,128)(2,1)} slice(bf16[6,26,24,768]{3,2,1,0:T(8,128)(2,1)S(1)} %select_maximum_fusion), slice={[0:6], [1:25], [0:24], [0:768]} | slice | bytes 10616832 | tf_op jit(solution)/shard_map/slice | solution.py:37
  186.1 1.5 copy.16
  187.6 17.1 %terms_first.1.refs_3_ = bf16[28,256,256]{2,1,0:T(8,128)(2,1)} custom-call(bf16[6,624,768]{2,1,0:T(8,128)(2,1)} %bitcast.32, bf16[6,576,768]{2,1,0:T(8,128)(2,1)} %bitcast.36, bf16[256,2304]{1,0:T(8,128)(2,1)} %bitcast.45), custom_call_target="tpu_custom_call" | custom-call | tf_op jit(solution)/shard_map/terms_first/pallas_call | solution.py:312
  204.8 1.2 maximum_bitcast_fusion
  205.9 0.9 fusion.12
  206.9 0.4 select_maximum_fusion.2
  207.3 3.0 %slice.131 = bf16[6,24,24,768]{3,2,1,0:T(8,128)(2,1)} slice(bf16[6,26,24,768]{3,2,1,0:T(8,128)(2,1)S(1)} %select_maximum_fusion.2), slice={[0:6], [1:25], [0:24], [0:768]} | slice | bytes 10616832 | tf_op jit(solution)/shard_map/slice | solution.py:37
  210.3 1.3 copy-done.2
  211.6 59.4 %grad_input.1 = (bf16[4,576,256]{2,1,0:T(8,128)(2,1)}, f32[28,32,256]{2,1,0:T(8,128)}) custom-call(bf16[6,624,768]{2,1,0:T(8,128)(2,1)} %bitcast.33, bf16[6,576,768]{2,1,0:T(8,128)(2,1)} %bitcast.38, bf16[256,7168]{1,0:T(8,128)(2,1)} %get-tuple-element.13.refs_2_, bf16[28,256,256]{2,1,0:T(8,128)(2,1)} %terms_first.1.refs_3_), custom_call_target="tpu_custom_call" | custom-call | tf_op jit(solution)/shard_map/grad_input/pallas_call | solution.py:312
  271.0 2.2 multiply_bitcast_fusion.1
  273.2 2.4 copy.20
  (23 shorter events, 0.1 us)
Async XLA Ops:
  0.6 2.3 copy-start.5
  3.0 4.4 %collective-permute-start.1 = (bf16[3,4,1,24,256]{4,3,2,1,0:T(8,128)(2,1)S(1)}, bf16[3,4,1,24,256]{4,3,2,1,0:T(8,128)(2,1)S(1)}, u32[]{:S(2)}, u32[]{:S(2)}) collective-permute-start(bf16[3,4,1,24,256]{4,3,2,1,0:T(8,128)(2,1)S(1)} %get-tuple-element.23), channel_id=1, source_target_pairs={{2,0},{3,1},{6,4},{7,5},{10,8},{11,9},{14,12},{15,13},{18,16},{19,... | collective-permute-start | bytes 442376 | tf_op jit(solution)/shard_map/ppermute | solution.py:24
  4.3 4.0 %collective-permute-start = (bf16[3,4,1,24,256]{4,3,2,1,0:T(8,128)(2,1)S(1)}, bf16[3,4,1,24,256]{4,3,2,1,0:T(8,128)(2,1)S(1)}, u32[]{:S(2)}, u32[]{:S(2)}) collective-permute-start(bf16[3,4,1,24,256]{4,3,2,1,0:T(8,128)(2,1)S(1)} %get-tuple-element.22), channel_id=1, source_target_pairs={{0,2},{1,3},{4,6},{5,7},{8,10},{9,11},{12,14},{13,15},{16,18},{17,... | collective-permute-start | bytes 442376 | tf_op jit(solution)/shard_map/ppermute | solution.py:21
  7.4 1.0 copy-start.7
  8.3 1.4 copy-start.9
  9.8 12.8 %collective-permute-start.3 = (bf16[3,4,26,1,256]{4,3,2,1,0:T(2,128)(2,1)}, bf16[3,4,26,1,256]{4,3,2,1,0:T(2,128)(2,1)}, u32[]{:S(2)}, u32[]{:S(2)}) collective-permute-start(bf16[3,4,26,1,256]{4,3,2,1,0:T(2,128)(2,1)} %get-tuple-element.21), channel_id=1, source_target_pairs={{1,0},{3,2},{5,4},{7,6},{9,8},{11,10},{13,12},{15,14},{17,16},{19,... | collective-permute-start | bytes 479240 | tf_op jit(solution)/shard_map/ppermute | solution.py:24
  11.1 13.2 %collective-permute-start.2 = (bf16[3,4,26,1,256]{4,3,2,1,0:T(2,128)(2,1)}, bf16[3,4,26,1,256]{4,3,2,1,0:T(2,128)(2,1)}, u32[]{:S(2)}, u32[]{:S(2)}) collective-permute-start(bf16[3,4,26,1,256]{4,3,2,1,0:T(2,128)(2,1)} %get-tuple-element.20), channel_id=1, source_target_pairs={{0,1},{2,3},{4,5},{6,7},{8,9},{10,11},{12,13},{14,15},{16,17},{18,... | collective-permute-start | bytes 479240 | tf_op jit(solution)/shard_map/ppermute | solution.py:21
  18.9 5.4 %copy-start.8 = (bf16[3,4,1,24,256]{4,3,2,1,0:T(8,128)(2,1)S(1)}, bf16[3,4,1,24,256]{4,3,2,1,0:T(8,128)(2,1)}, u32[]{:S(2)}) copy-start(bf16[3,4,1,24,256]{4,3,2,1,0:T(8,128)(2,1)} %copy-done.7) | copy-start | bytes 442372
  18.9 5.4 %copy-start.10 = (bf16[3,4,1,24,256]{4,3,2,1,0:T(8,128)(2,1)S(1)}, bf16[3,4,1,24,256]{4,3,2,1,0:T(8,128)(2,1)}, u32[]{:S(2)}) copy-start(bf16[3,4,1,24,256]{4,3,2,1,0:T(8,128)(2,1)} %copy-done.9) | copy-start | bytes 442372
  31.1 4.1 %copy-start = (bf16[6,26,24,768]{3,2,1,0:T(8,128)(2,1)}, bf16[6,26,24,768]{3,2,1,0:T(8,128)(2,1)S(1)}, u32[]{:S(2)}) copy-start(bf16[6,26,24,768]{3,2,1,0:T(8,128)(2,1)S(1)} %fusion.8) | copy-start | bytes 17252356
  36.6 4.2 %copy-start.3 = (bf16[6,26,24,768]{3,2,1,0:T(8,128)(2,1)}, bf16[6,26,24,768]{3,2,1,0:T(8,128)(2,1)S(1)}, u32[]{:S(2)}) copy-start(bf16[6,26,24,768]{3,2,1,0:T(8,128)(2,1)S(1)} %fusion.10) | copy-start | bytes 17252356
  169.6 5.9 %collective-permute-start.5 = (bf16[1,4,1,24,256]{4,3,2,1,0:T(8,128)(2,1)S(1)}, bf16[1,4,1,24,256]{4,3,2,1,0:T(8,128)(2,1)S(1)}, u32[]{:S(2)}, u32[]{:S(2)}) collective-permute-start(bf16[1,4,1,24,256]{4,3,2,1,0:T(8,128)(2,1)S(1)} %get-tuple-element.39), channel_id=1, source_target_pairs={{2,0},{3,1},{6,4},{7,5},{10,8},{11,9},{14,12},{15,13},{18,16},{19,... | collective-permute-start | bytes 147464 | tf_op jit(solution)/shard_map/ppermute | solution.py:24
  170.9 4.6 %collective-permute-start.4 = (bf16[1,4,1,24,256]{4,3,2,1,0:T(8,128)(2,1)S(1)}, bf16[1,4,1,24,256]{4,3,2,1,0:T(8,128)(2,1)S(1)}, u32[]{:S(2)}, u32[]{:S(2)}) collective-permute-start(bf16[1,4,1,24,256]{4,3,2,1,0:T(8,128)(2,1)S(1)} %get-tuple-element.38), channel_id=1, source_target_pairs={{0,2},{1,3},{4,6},{5,7},{8,10},{9,11},{12,14},{13,15},{16,18},{17,... | collective-permute-start | bytes 147464 | tf_op jit(solution)/shard_map/ppermute | solution.py:21
  175.0 1.3 copy-start.4
  175.0 7.3 %copy-start.6 = (f32[28,32,256]{2,1,0:T(8,128)S(1)}, f32[28,32,256]{2,1,0:T(8,128)}, u32[]{:S(2)}) copy-start(f32[28,32,256]{2,1,0:T(8,128)} %get-tuple-element.16) | copy-start | bytes 2752516
  175.5 10.6 %copy-start.1 = (bf16[6,26,24,768]{3,2,1,0:T(8,128)(2,1)}, bf16[6,26,24,768]{3,2,1,0:T(8,128)(2,1)S(1)}, u32[]{:S(2)}) copy-start(bf16[6,26,24,768]{3,2,1,0:T(8,128)(2,1)S(1)} %select_maximum_fusion) | copy-start | bytes 17252356
  176.4 28.3 %collective-permute-start.7 = (bf16[1,4,26,1,256]{4,3,2,1,0:T(2,128)(2,1)S(1)}, bf16[1,4,26,1,256]{4,3,2,1,0:T(2,128)(2,1)S(1)}, u32[]{:S(2)}, u32[]{:S(2)}) collective-permute-start(bf16[1,4,26,1,256]{4,3,2,1,0:T(2,128)(2,1)S(1)} %get-tuple-element.37), channel_id=1, source_target_pairs={{1,0},{3,2},{5,4},{7,6},{9,8},{11,10},{13,12},{15,14},{17,16},{19,... | collective-permute-start | bytes 159752 | tf_op jit(solution)/shard_map/ppermute | solution.py:24
  177.7 27.0 %collective-permute-start.6 = (bf16[1,4,26,1,256]{4,3,2,1,0:T(2,128)(2,1)S(1)}, bf16[1,4,26,1,256]{4,3,2,1,0:T(2,128)(2,1)S(1)}, u32[]{:S(2)}, u32[]{:S(2)}) collective-permute-start(bf16[1,4,26,1,256]{4,3,2,1,0:T(2,128)(2,1)S(1)} %get-tuple-element.36), channel_id=1, source_target_pairs={{0,1},{2,3},{4,5},{6,7},{8,9},{10,11},{12,13},{14,15},{16,17},{18,... | collective-permute-start | bytes 159752 | tf_op jit(solution)/shard_map/ppermute | solution.py:21
  207.3 4.3 %copy-start.2 = (bf16[6,26,24,768]{3,2,1,0:T(8,128)(2,1)}, bf16[6,26,24,768]{3,2,1,0:T(8,128)(2,1)S(1)}, u32[]{:S(2)}) copy-start(bf16[6,26,24,768]{3,2,1,0:T(8,128)(2,1)S(1)} %select_maximum_fusion.2) | copy-start | bytes 17252356

commit v2 on v1

v2 whole, which is shorter than its diff:
```python
import functools
import math

import jax
import jax.numpy as jnp
from jax import lax
from jax.experimental import pallas as pl
from jax.experimental.pallas import tpu as pltpu
from jax.sharding import PartitionSpec as P

MESH = pl.DeviceIdType.MESH
VMEM = pl.BlockSpec(memory_space=pltpu.VMEM)
NT = (((1,), (1,)), ((), ()))


def extended(block, sides, width):
    for axis, dim in sides:
        count = lax.axis_size(axis)
        forward = [(i, i + 1) for i in range(count - 1)]
        backward = [(target, source) for source, target in forward]
        low = lax.ppermute(
            lax.slice_in_dim(block, block.shape[dim] - width, None, axis=dim), axis, forward
        )
        high = lax.ppermute(lax.slice_in_dim(block, 0, width, axis=dim), axis, backward)
        block = jnp.concatenate([low, block, high], axis=dim)
    return block


def shifted_views(field, order):
    depth, high, wide, _ = field.shape
    high, wide = high - 2, wide - 2
    lanes = jnp.concatenate([field[:, :, c : c + wide, :] for c in order], axis=-1)
    lanes = jnp.pad(lanes, ((1, 1), (0, 0), (0, 0), (0, 0)))
    if (2 * wide) % 16 == 0:
        return [
            lanes.reshape(depth + 2, (high + 2) * wide, -1),
            lanes[:, 1 : 1 + high].reshape(depth + 2, high * wide, -1),
        ]
    return [lanes[:, b : b + high].reshape(depth + 2, high * wide, -1) for b in range(3)]


def view_at(views, b, pitch):
    if len(views) == 2:
        return (views[1], 0) if b == 1 else (views[0], b * pitch)
    return views[b], 0


def filter_group(views, pitch, grad_t, out, b):
    ch, rows = grad_t.shape
    depth = views[0].shape[0] - 2
    plane = rows // depth
    view, start = view_at(views, b, pitch)

    def step(a, _):
        block = view[pl.ds(a, depth), start : start + plane, :].reshape(rows, -1)
        acc = jnp.dot(grad_t[...], block, preferred_element_type=jnp.float32)
        for c in range(3):
            out[9 * b + 3 * a + c] = acc[:, c * ch : (c + 1) * ch].T.astype(out.dtype)
        return 0

    lax.fori_loop(0, 3, step, 0)


def data_plane(views, pitch, weight, acc, x):
    plane, ch = acc.shape
    acc[...] = jnp.zeros_like(acc)

    def step(a, _):
        total = None
        for b in range(3):
            view, start = view_at(views, 2 - b, pitch)
            block = view[x + 2 - a, start : start + plane, :]
            first = pl.multiple_of((9 * a + 3 * b) * ch, 128)
            term = lax.dot_general(
                block,
                weight[:, pl.ds(first, 3 * ch)],
                NT,
                preferred_element_type=jnp.float32,
            )
            total = term if total is None else total + term
        acc[...] += total
        return 0

    lax.fori_loop(0, 3, step, 0)


def enter(sizes):
    barrier = pltpu.get_barrier_semaphore()
    count = 0
    for axis, size in sizes.items():
        me = lax.axis_index(axis)
        for d in range(1, size):
            pl.semaphore_signal(
                barrier, inc=1, device_id={axis: lax.rem(me + d, size)}, device_id_type=MESH
            )
            count += 1
    pl.semaphore_wait(barrier, count)


def fan_out(axis, size, source, target, send, recv):
    me = lax.axis_index(axis)
    copies = []
    for d in range(1, size):
        peer = lax.rem(me + d, size)
        copies.append(
            pltpu.make_async_remote_copy(
                src_ref=source(peer),
                dst_ref=target(d),
                send_sem=send.at[d],
                recv_sem=recv.at[d],
                device_id={axis: peer},
                device_id_type=MESH,
            )
        )
    for copy in copies:
        copy.start()
    return copies


def gather_stages(sizes, shard, whole, sems, first, width, over_tiles):
    ndp, nty, ntz = sizes["dp"], sizes["ty"], sizes["tz"]
    dp, ty, tz = lax.axis_index("dp"), lax.axis_index("ty"), lax.axis_index("tz")
    rows = shard.shape[0]
    span = width // nty
    part = span // ntz if over_tiles else span
    start = first + ty * span
    group = pl.ds(pl.multiple_of(start, 128), span)
    mine = pl.ds(pl.multiple_of(start + tz * part, 128), part) if over_tiles else group
    own = pl.ds(pl.multiple_of(dp * rows, 16), rows)

    whole[own, mine] = shard[:, mine]
    copies = fan_out(
        "dp", ndp, lambda peer: shard.at[:, mine], lambda d: whole.at[own, mine], sems.at[0], sems.at[1]
    )
    yield
    for copy in copies:
        copy.wait()
    if over_tiles:
        copies = fan_out(
            "tz", ntz, lambda peer: whole.at[:, mine], lambda d: whole.at[:, mine], sems.at[2], sems.at[3]
        )
        yield
        for copy in copies:
            copy.wait()
    copies = fan_out(
        "ty", nty, lambda peer: whole.at[:, group], lambda d: whole.at[:, group], sems.at[4], sems.at[5]
    )
    yield
    for copy in copies:
        copy.wait()


def added(count, own, others, store):
    def step(t, _):
        total = own(t).astype(jnp.float32)
        for d in range(others.shape[0]):
            total += others[d, t].astype(jnp.float32)
        store(t, total)
        return 0

    lax.fori_loop(0, count, step, 0)


def reduce_stages(sizes, part, out, bufs, sems, first, tz_first):
    ndp, nty, ntz = sizes["dp"], sizes["ty"], sizes["tz"]
    dp, ty, tz = lax.axis_index("dp"), lax.axis_index("ty"), lax.axis_index("tz")
    over_ty, sum_ty, over_tz, second, over_dp = bufs
    wide, rows = sum_ty.shape[0], over_dp.shape[2]
    few = wide // ntz
    begin = first + ty * wide
    slot = begin + tz * few
    own = pl.ds(pl.multiple_of(dp * rows, 16), rows)

    def rows_of(peer):
        return pl.ds(pl.multiple_of(peer * rows, 16), rows)

    def put(target, offset):
        def store(t, total):
            target[offset + t] = total.astype(target.dtype)

        return store

    copies = fan_out(
        "ty", nty, lambda peer: part.at[pl.ds(first + peer * wide, wide)], lambda d: over_ty.at[d - 1],
        sems.at[0], sems.at[1],
    )
    yield
    for copy in copies:
        copy.wait()
    added(wide, lambda t: part[begin + t], over_ty, put(sum_ty, 0))
    if tz_first:
        copies = fan_out(
            "tz", ntz, lambda peer: sum_ty.at[pl.ds(peer * few, few)], lambda d: over_tz.at[d - 1],
            sems.at[2], sems.at[3],
        )
        yield
        for copy in copies:
            copy.wait()
        added(few, lambda t: sum_ty[tz * few + t], over_tz, put(second, 0))
        copies = fan_out(
            "dp", ndp, lambda peer: second.at[:, rows_of(peer)], lambda d: over_dp.at[d - 1],
            sems.at[4], sems.at[5],
        )
        yield
        for copy in copies:
            copy.wait()
        added(few, lambda t: second[t, own], over_dp, put(out, slot))
    else:
        copies = fan_out(
            "dp", ndp, lambda peer: sum_ty.at[:, rows_of(peer)], lambda d: over_dp.at[d - 1],
            sems.at[4], sems.at[5],
        )
        yield
        for copy in copies:
            copy.wait()
        added(wide, lambda t: sum_ty[t, own], over_dp, put(second, 0))
        copies = fan_out(
            "tz", ntz, lambda peer: second.at[pl.ds(peer * few, few)], lambda d: over_tz.at[d - 1],
            sems.at[2], sems.at[3],
        )
        yield
        for copy in copies:
            copy.wait()
        added(few, lambda t: second[tz * few + t], over_tz, put(out, slot))
    mine = out.at[pl.ds(slot, few)]
    copies = fan_out("tz", ntz, lambda peer: mine, lambda d: mine, sems.at[6], sems.at[7])
    yield
    for copy in copies:
        copy.wait()
    group = out.at[pl.ds(begin, wide)]
    copies = fan_out("ty", nty, lambda peer: group, lambda d: group, sems.at[8], sems.at[9])
    yield
    for copy in copies:
        copy.wait()


def advance(stages):
    done = object()
    return [stage for stage in stages if next(stage, done) is not done]


def chains_of(tiles):
    if tiles == 4:
        return [(8, 0, True), (8, 1, False), (8, 2, True), (4, 2, False)]
    return [(16, 1, True), (16, 2, False)]


def layer_kernel(sizes, pitch, count, masked, *refs):
    refs = list(refs)

    def take(n):
        taken = refs[:n]
        del refs[:n]
        return taken

    field_views, data_hbm = take(count), take(count)
    grad_t, shard = take(2)
    pre = take(1)[0] if masked else None
    grad, reduced = take(2)
    data_views = take(count)
    terms, whole, acc, copy_sems, gather_sems, reduce_sems = take(6)

    loads = [
        pltpu.make_async_copy(source, target, copy_sems.at[n])
        for n, (source, target) in enumerate(zip(data_hbm, data_views))
    ]
    for load in loads:
        load.start()
    enter(sizes)
    half = 16 * grad_t.shape[0]
    lanes = shard.shape[1]
    gathers = [
        gather_stages(sizes, shard, whole, gather_sems.at[0], 0, half, True),
        gather_stages(sizes, shard, whole, gather_sems.at[1], half, lanes - half, False),
    ]
    gathers = advance(gathers)
    for tap in range(27, terms.shape[0]):
        terms[tap] = jnp.zeros(terms.shape[1:], terms.dtype)
    reductions = []
    for b in range(3):
        filter_group(field_views, pitch, grad_t, terms, b)
        gathers, reductions = advance(gathers), advance(reductions)
        first = 0
        for n, (slots, after, tz_first) in enumerate(chains_of(sizes["ty"] * sizes["tz"])):
            if after == b:
                bufs = refs[5 * n : 5 * n + 5]
                reductions += advance(
                    [reduce_stages(sizes, terms, reduced, bufs, reduce_sems.at[n], first, tz_first)]
                )
            first += slots
    while gathers:
        gathers = advance(gathers)
    for load in loads:
        load.wait()
    for x in range(grad.shape[0]):
        data_plane(data_views, pitch, whole, acc, x)
        value = acc[...]
        if masked:
            value = jnp.where(pre[x].astype(jnp.float32) > 0, value, 0.0)
        grad[x] = value.astype(grad.dtype)
        reductions = advance(reductions)
    while reductions:
        reductions = advance(reductions)


def local(inputs, pre_first, pre_second, grad_out, w_first, w_second):
    frames, depth, high, wide, ch = grad_out.shape
    sizes = {axis: lax.axis_size(axis) for axis in ("dp", "ty", "tz")}
    ndp, nty, ntz = sizes["dp"], sizes["ty"], sizes["tz"]
    tiles = nty * ntz
    scale = 1.0 / math.sqrt(frames * depth * high * wide * ndp * tiles)
    sides = (("ty", 2), ("tz", 3))
    half = jnp.bfloat16
    rows, plane = depth * high * wide, high * wide
    taps = -(-27 // tiles) * tiles
    share = ch // ndp
    lanes = taps * ch
    shape = jax.ShapeDtypeStruct
    dma = pltpu.SemaphoreType.DMA

    zero_half = jnp.zeros((), half)
    grad_top = jnp.where(pre_second > 0, grad_out, zero_half)
    active = jnp.where(pre_first > 0, pre_first, zero_half)
    padded = extended(jnp.concatenate([active, grad_top, inputs], axis=0), sides, 1)
    forward, backward = (0, 1, 2), (2, 1, 0)
    act_views = shifted_views(padded[0], forward)
    top_views = shifted_views(padded[1], backward)
    in_views = shifted_views(padded[2], forward)
    count = len(act_views)
    shards = [
        jnp.pad(w.reshape(share, -1), ((0, 0), (0, lanes - 27 * ch))) for w in (w_second, w_first)
    ]

    chains = chains_of(tiles)
    most = max(sizes.values())
    scratch = [
        pltpu.VMEM((taps, ch, ch), half),
        pltpu.VMEM((ch, lanes), half),
        pltpu.VMEM((plane, ch), jnp.float32),
        dma((count,)),
        dma((2, 6, most)),
        dma((len(chains), 10, most)),
    ]
    for slots, _, tz_first in chains:
        across = slots // nty
        little = across // ntz
        scratch += [
            pltpu.VMEM((nty - 1, across, ch, ch), half),
            pltpu.VMEM((across, ch, ch), half),
            pltpu.VMEM((ntz - 1, little, ch if tz_first else share, ch), half),
            pltpu.VMEM((little, ch, ch) if tz_first else (across, share, ch), half),
            pltpu.VMEM((ndp - 1, little if tz_first else across, share, ch), half),
        ]
    anywhere = pl.BlockSpec(memory_space=pl.ANY)

    def layer(name, collective_id, field_views, data_views, grad, shard, pre):
        operands = [*field_views, *data_views, grad.reshape(rows, ch).T, shard]
        masked = pre is not None
        if masked:
            operands.append(pre.reshape(depth, plane, ch))
        in_specs = [VMEM] * len(operands)
        in_specs[count : 2 * count] = [anywhere] * count
        return pl.pallas_call(
            functools.partial(layer_kernel, sizes, wide, count, masked),
            out_shape=(shape((depth, plane, ch), half), shape((taps, share, ch), half)),
            in_specs=in_specs,
            out_specs=(VMEM, VMEM),
            scratch_shapes=[pltpu.VMEM(v.shape, half) for v in data_views] + scratch,
            compiler_params=pltpu.CompilerParams(
                vmem_limit_bytes=58 * 1024 * 1024, collective_id=collective_id, has_side_effects=True
            ),
            name=name,
        )(*operands)

    grad_low, reduced_second = layer(
        "second_layer", 0, act_views, top_views, grad_top, shards[0], pre_first
    )
    low_views = shifted_views(
        extended(grad_low.reshape(1, depth, high, wide, ch), sides, 1)[0], backward
    )
    grad_input, reduced_first = layer(
        "first_layer", 1, in_views, low_views, grad_low, shards[1], None
    )

    def filter_out(reduced):
        whole = reduced[:27].reshape(3, 3, 3, share, ch).transpose(3, 1, 0, 2, 4)
        return whole.reshape(share, 27, ch).astype(jnp.float32) * scale

    return (
        grad_input.reshape(grad_out.shape),
        filter_out(reduced_first),
        filter_out(reduced_second),
    )


def solution(mesh):
    placed = (
        P("dp", None, "ty", "tz", None),
        P("dp", None, "ty", "tz", None),
        P("dp", None, "ty", "tz", None),
        P("dp", None, "ty", "tz", None),
        P("dp", None, None),
        P("dp", None, None),
    )
    return jax.shard_map(
        local,
        mesh=mesh,
        in_specs=placed,
        out_specs=(P("dp", None, "ty", "tz", None), P("dp", None, None), P("dp", None, None)),
        check_vma=False,
    )
```

time: 280 us -> 249 us (0.89); the launches traced: 276 us -> 248 us
  Pallas kernels: 204 us -> 174 us
  starting transfers between devices: 22.2 us -> 17.7 us
  waiting for transfers between devices: 2.6 us -> 6.9 us
    pallas_call x4 -> x2, Pallas kernels: 204 us -> 174 us  [layer(): pl.pallas_call(functools.partial(layer_kernel, sizes, wide, count, masked...]
    ppermute x4, waiting for transfers between devices: 0.01 us -> 6.78 us  [extended(): lax.ppermute(lax.slice_in_dim(block, 0, width, axis=dim), axis, backward)]
    ppermute x4, starting transfers between devices: 17.1 us -> 12.5 us  [extended(): lax.ppermute(lax.slice_in_dim(block, block.shape[dim] - width, None, axis...]
  transfers between devices with their start and end apart: 8 -> 8, of which waited for: 2 -> 3; matrix products, arithmetic and copies ran while one was open for 4% -> 7% of each run, Pallas kernels for 6% -> 0%
where the time goes in v2:
time: 249 us; the launch traced here: 248 us
  Pallas kernels  174 us (70%)
  local copies, waits for them, and re-layouts  32.7 us (13%)
  starting transfers between devices  17.7 us (7%)
  other arithmetic  15.5 us (6%)
  waiting for transfers between devices  6.9 us (3%)
    pallas_call x2, Pallas kernels, layer(): pl.pallas_call(functools.partial(layer_kernel, sizes, wide, count, masked...  174 us
    slice x4, local copies, waits for them, and re-layouts, shifted_views(): lanes[:, 1:1 + high].reshape(depth + 2, high * wide, -1)  13.9 us
    ppermute x4, starting transfers between devices, extended(): lax.ppermute(lax.slice_in_dim(block, block.shape[dim] - width, None, axis...  12.5 us
    ppermute x4, waiting for transfers between devices, extended(): lax.ppermute(lax.slice_in_dim(block, 0, width, axis=dim), axis, backward)  6.78 us
    ppermute x4, starting transfers between devices, extended(): lax.ppermute(lax.slice_in_dim(block, 0, width, axis=dim), axis, backward)  5.16 us
  transfers between devices with their start and end apart: 8, of which 3 were waited for; matrix products, arithmetic and copies ran while one was open for 7% of the time, Pallas kernels for 0%

profile of v2, /device:TPU:0, one launch (start us, length us, event | category | flops | bytes accessed | tf_op | source)
XLA Modules:
  0.0 248.1 jit_solution(9060838376061354707)
XLA Ops:
  0.6 2.3 compare_select_fusion
  2.9 0.0 copy-done.4
  3.0 2.4 collective-permute-start
  5.4 1.3 collective-permute-start.1
  6.7 0.0 collective-permute-done
  6.7 1.9 collective-permute-done.1
  8.6 1.4 pad_maximum_fusion.5
  10.1 5.0 %collective-permute-start.2 = (bf16[3,4,26,1,256]{4,3,2,1,0:T(2,128)(2,1)}, bf16[3,4,26,1,256]{4,3,2,1,0:T(2,128)(2,1)}, u32[]{:S(2)}, u32[]{:S(2)}) collective-permute-start(bf16[3,4,26,1,256]{4,3,2,1,0:T(2,128)(2,1)} %get-tuple-element.14), channel_id=1, source_target_pairs={{0,1},{2,3},{4,5},{6,7},{8,9},{10,11},{12,13},{14,15},{16,17},{18,... | collective-permute-start | bytes 479240 | tf_op jit(solution)/shard_map/ppermute | solution.py:21
  15.0 1.3 collective-permute-start.3
  16.3 1.5 copy.15
  17.9 1.1 copy.21
  19.0 1.0 copy.22
  20.0 0.8 pad.23.refs_5_
  20.8 0.8 pad.25.refs_5_
  21.6 0.1 collective-permute-done.2
  21.7 4.8 %collective-permute-done.3 = bf16[3,4,26,1,256]{4,3,2,1,0:T(2,128)(2,1)} collective-permute-done((bf16[3,4,26,1,256]{4,3,2,1,0:T(2,128)(2,1)}, bf16[3,4,26,1,256]{4,3,2,1,0:T(2,128)(2,1)}, u32[]{:S(2)}, u32[]{:S(2)}) %collective-permute-start.3) | collective-permute-done | bytes 159776 | tf_op jit(solution)/shard_map/ppermute | solution.py:24
  26.6 4.8 %pad_maximum_fusion = bf16[3,4,26,26,256]{4,3,2,1,0:T(8,128)(2,1)S(1)} fusion(bf16[3,4,26,1,256]{4,3,2,1,0:T(2,128)(2,1)} %collective-permute-done.3, bf16[3,4,1,24,256]{4,3,2,1,0:T(8,128)(2,1)S(1)} %copy-done.9, bf16[1,4,24,24,256]{4,3,2,1,0:T(8,128)(2,1)S(1)} %copy-done.4, bf16[1,4,24,24,256]{4,3,2,1,0:T(8,128)(2,1)S(1)} %get-tuple-element.35, ...), kind=kLoop, calls=%fused_computation.11 | loop fusion | flops 29073408 | bytes 8306688 | tf_op jit(solution)/shard_map/concatenate | solution.py:25
  31.3 0.6 slice_bitcast_fusion
  32.0 0.9 fusion.2
  32.9 0.4 select_maximum_fusion.2
  33.4 2.9 %slice.130 = bf16[6,24,24,768]{3,2,1,0:T(8,128)(2,1)} slice(bf16[6,26,24,768]{3,2,1,0:T(8,128)(2,1)S(1)} %select_maximum_fusion.2), slice={[0:6], [1:25], [0:24], [0:768]} | slice | bytes 10616832 | tf_op jit(solution)/shard_map/slice | solution.py:37
  36.3 1.3 copy-done
  37.6 1.0 fusion.3
  38.5 0.4 select_maximum_fusion.4
  39.0 2.9 %slice.125 = bf16[6,24,24,768]{3,2,1,0:T(8,128)(2,1)} slice(bf16[6,26,24,768]{3,2,1,0:T(8,128)(2,1)S(1)} %select_maximum_fusion.4), slice={[0:6], [1:25], [0:24], [0:768]} | slice | bytes 10616832 | tf_op jit(solution)/shard_map/slice | solution.py:37
  41.9 1.2 copy-done.1
  43.1 86.6 %second_layer.1 = (bf16[4,576,256]{2,1,0:T(8,128)(2,1)}, bf16[28,32,256]{2,1,0:T(8,128)(2,1)}) custom-call(bf16[6,624,768]{2,1,0:T(8,128)(2,1)} %bitcast.36, bf16[6,576,768]{2,1,0:T(8,128)(2,1)} %bitcast.42, bf16[6,624,768]{2,1,0:T(8,128)(2,1)} %bitcast.35, bf16[6,576,768]{2,1,0:T(8,128)(2,1)} %bitcast.41, bf16[256,2304]{1,0:T(8,128)(2,1)} %bitcast.48, ...), custom_call_target="tpu_custom_call" | custom-call | tf_op jit(solution)/shard_map/second_layer/pallas_call | solution.py:363
  129.7 0.8 fusion.5
  130.6 2.2 collective-permute-start.4
  132.8 1.3 collective-permute-start.5
  134.1 0.9 fusion.4
  135.0 3.0 %select_maximum_fusion.6 = bf16[6,26,24,768]{3,2,1,0:T(8,128)(2,1)} fusion(bf16[4,26,24,256]{3,2,1,0:T(8,128)(2,1)S(1)} %get-tuple-element.28, bf16[4,26,24,256]{3,2,1,0:T(8,128)(2,1)S(1)} %get-tuple-element.29, bf16[4,26,24,256]{3,2,1,0:T(8,128)(2,1)S(1)} %get-tuple-element.27), kind=kLoop, calls=%fused_computation.9 | loop fusion | flops 34504704 | bytes 9584640 | tf_op jit(solution)/shard_map/concatenate | solution.py:32
  138.1 0.2 pad_maximum_fusion.11
  138.2 2.9 %collective-permute-start.6 = (bf16[1,4,26,1,256]{4,3,2,1,0:T(2,128)(2,1)S(1)}, bf16[1,4,26,1,256]{4,3,2,1,0:T(2,128)(2,1)S(1)}, u32[]{:S(2)}, u32[]{:S(2)}) collective-permute-start(bf16[1,4,26,1,256]{4,3,2,1,0:T(2,128)(2,1)S(1)} %get-tuple-element.30), channel_id=1, source_target_pairs={{0,1},{2,3},{4,5},{6,7},{8,9},{10,11},{12,13},{14,15},{16,17},{18,... | collective-permute-start | bytes 159752 | tf_op jit(solution)/shard_map/ppermute | solution.py:21
  141.2 1.3 collective-permute-start.7
  142.5 0.1 convert_multiply_fusion
  142.6 1.5 copy.17
  144.1 5.1 %slice.120 = bf16[6,24,24,768]{3,2,1,0:T(8,128)(2,1)} slice(bf16[6,26,24,768]{3,2,1,0:T(8,128)(2,1)} %select_maximum_fusion.6), slice={[0:6], [1:25], [0:24], [0:768]} | slice | bytes 10616832 | tf_op jit(solution)/shard_map/slice | solution.py:37
  149.3 1.0 copy.20
  150.2 1.2 maximum_bitcast_fusion
  151.4 0.9 fusion.1
  152.4 0.4 select_maximum_fusion
  152.8 2.9 %slice.136 = bf16[6,24,24,768]{3,2,1,0:T(8,128)(2,1)} slice(bf16[6,26,24,768]{3,2,1,0:T(8,128)(2,1)S(1)} %select_maximum_fusion), slice={[0:6], [1:25], [0:24], [0:768]} | slice | bytes 10616832 | tf_op jit(solution)/shard_map/slice | solution.py:37
  155.7 1.3 copy-done.2
  157.0 87.8 %first_layer.1 = (bf16[4,576,256]{2,1,0:T(8,128)(2,1)}, bf16[28,32,256]{2,1,0:T(8,128)(2,1)}) custom-call(bf16[6,624,768]{2,1,0:T(8,128)(2,1)} %bitcast.37, bf16[6,576,768]{2,1,0:T(8,128)(2,1)} %bitcast.40, bf16[6,624,768]{2,1,0:T(8,128)(2,1)} %bitcast.38, bf16[6,576,768]{2,1,0:T(8,128)(2,1)} %bitcast.43, bf16[256,2304]{1,0:T(8,128)(2,1)} %bitcast.49, ...), custom_call_target="tpu_custom_call" | custom-call | tf_op jit(solution)/shard_map/first_layer/pallas_call | solution.py:363
  244.8 1.2 convert_multiply_fusion.1
  246.1 1.0 copy.19
  247.1 1.0 copy.24
  (23 shorter events, 0.1 us)
Async XLA Ops:
  0.6 2.3 copy-start.4
  3.0 3.7 %collective-permute-start = (bf16[3,4,1,24,256]{4,3,2,1,0:T(8,128)(2,1)S(1)}, bf16[3,4,1,24,256]{4,3,2,1,0:T(8,128)(2,1)S(1)}, u32[]{:S(2)}, u32[]{:S(2)}) collective-permute-start(bf16[3,4,1,24,256]{4,3,2,1,0:T(8,128)(2,1)S(1)} %get-tuple-element.16), channel_id=1, source_target_pairs={{0,2},{1,3},{4,6},{5,7},{8,10},{9,11},{12,14},{13,15},{16,18},{17,... | collective-permute-start | bytes 442376 | tf_op jit(solution)/shard_map/ppermute | solution.py:21
  5.4 3.3 %collective-permute-start.1 = (bf16[3,4,1,24,256]{4,3,2,1,0:T(8,128)(2,1)S(1)}, bf16[3,4,1,24,256]{4,3,2,1,0:T(8,128)(2,1)S(1)}, u32[]{:S(2)}, u32[]{:S(2)}) collective-permute-start(bf16[3,4,1,24,256]{4,3,2,1,0:T(8,128)(2,1)S(1)} %get-tuple-element.17), channel_id=1, source_target_pairs={{2,0},{3,1},{6,4},{7,5},{10,8},{11,9},{14,12},{15,13},{18,16},{19,... | collective-permute-start | bytes 442376 | tf_op jit(solution)/shard_map/ppermute | solution.py:24
  6.7 2.0 copy-start.6
  8.6 1.4 copy-start.8
  10.1 11.6 %collective-permute-start.2 = (bf16[3,4,26,1,256]{4,3,2,1,0:T(2,128)(2,1)}, bf16[3,4,26,1,256]{4,3,2,1,0:T(2,128)(2,1)}, u32[]{:S(2)}, u32[]{:S(2)}) collective-permute-start(bf16[3,4,26,1,256]{4,3,2,1,0:T(2,128)(2,1)} %get-tuple-element.14), channel_id=1, source_target_pairs={{0,1},{2,3},{4,5},{6,7},{8,9},{10,11},{12,13},{14,15},{16,17},{18,... | collective-permute-start | bytes 479240 | tf_op jit(solution)/shard_map/ppermute | solution.py:21
  15.0 11.5 %collective-permute-start.3 = (bf16[3,4,26,1,256]{4,3,2,1,0:T(2,128)(2,1)}, bf16[3,4,26,1,256]{4,3,2,1,0:T(2,128)(2,1)}, u32[]{:S(2)}, u32[]{:S(2)}) collective-permute-start(bf16[3,4,26,1,256]{4,3,2,1,0:T(2,128)(2,1)} %get-tuple-element.15), channel_id=1, source_target_pairs={{1,0},{3,2},{5,4},{7,6},{9,8},{11,10},{13,12},{15,14},{17,16},{19,... | collective-permute-start | bytes 479240 | tf_op jit(solution)/shard_map/ppermute | solution.py:24
  17.9 8.7 %copy-start.7 = (bf16[3,4,1,24,256]{4,3,2,1,0:T(8,128)(2,1)S(1)}, bf16[3,4,1,24,256]{4,3,2,1,0:T(8,128)(2,1)}, u32[]{:S(2)}) copy-start(bf16[3,4,1,24,256]{4,3,2,1,0:T(8,128)(2,1)} %copy-done.6) | copy-start | bytes 442372
  17.9 8.7 %copy-start.9 = (bf16[3,4,1,24,256]{4,3,2,1,0:T(8,128)(2,1)S(1)}, bf16[3,4,1,24,256]{4,3,2,1,0:T(8,128)(2,1)}, u32[]{:S(2)}) copy-start(bf16[3,4,1,24,256]{4,3,2,1,0:T(8,128)(2,1)} %copy-done.8) | copy-start | bytes 442372
  33.4 4.2 %copy-start = (bf16[6,26,24,768]{3,2,1,0:T(8,128)(2,1)}, bf16[6,26,24,768]{3,2,1,0:T(8,128)(2,1)S(1)}, u32[]{:S(2)}) copy-start(bf16[6,26,24,768]{3,2,1,0:T(8,128)(2,1)S(1)} %select_maximum_fusion.2) | copy-start | bytes 17252356
  39.0 4.1 %copy-start.1 = (bf16[6,26,24,768]{3,2,1,0:T(8,128)(2,1)}, bf16[6,26,24,768]{3,2,1,0:T(8,128)(2,1)S(1)}, u32[]{:S(2)}) copy-start(bf16[6,26,24,768]{3,2,1,0:T(8,128)(2,1)S(1)} %select_maximum_fusion.4) | copy-start | bytes 17252356
  130.6 7.5 %collective-permute-start.4 = (bf16[1,4,1,24,256]{4,3,2,1,0:T(8,128)(2,1)S(1)}, bf16[1,4,1,24,256]{4,3,2,1,0:T(8,128)(2,1)S(1)}, u32[]{:S(2)}, u32[]{:S(2)}) collective-permute-start(bf16[1,4,1,24,256]{4,3,2,1,0:T(8,128)(2,1)S(1)} %get-tuple-element.32), channel_id=1, source_target_pairs={{0,2},{1,3},{4,6},{5,7},{8,10},{9,11},{12,14},{13,15},{16,18},{17,... | collective-permute-start | bytes 147464 | tf_op jit(solution)/shard_map/ppermute | solution.py:21
  132.8 5.2 %collective-permute-start.5 = (bf16[1,4,1,24,256]{4,3,2,1,0:T(8,128)(2,1)S(1)}, bf16[1,4,1,24,256]{4,3,2,1,0:T(8,128)(2,1)S(1)}, u32[]{:S(2)}, u32[]{:S(2)}) collective-permute-start(bf16[1,4,1,24,256]{4,3,2,1,0:T(8,128)(2,1)S(1)} %get-tuple-element.33), channel_id=1, source_target_pairs={{2,0},{3,1},{6,4},{7,5},{10,8},{11,9},{14,12},{15,13},{18,16},{19,... | collective-permute-start | bytes 147464 | tf_op jit(solution)/shard_map/ppermute | solution.py:24
  135.0 3.0 %copy-start.3 = (bf16[4,576,256]{2,1,0:T(8,128)(2,1)S(1)}, bf16[4,576,256]{2,1,0:T(8,128)(2,1)}, u32[]{:S(2)}) copy-start(bf16[4,576,256]{2,1,0:T(8,128)(2,1)} %get-tuple-element.7) | copy-start | bytes 3538948
  135.0 7.4 %copy-start.10 = (bf16[28,32,256]{2,1,0:T(8,128)(2,1)S(1)}, bf16[28,32,256]{2,1,0:T(8,128)(2,1)}, u32[]{:S(2)}) copy-start(bf16[28,32,256]{2,1,0:T(8,128)(2,1)} %get-tuple-element.10) | copy-start | bytes 1376260
  138.2 12.0 %collective-permute-start.6 = (bf16[1,4,26,1,256]{4,3,2,1,0:T(2,128)(2,1)S(1)}, bf16[1,4,26,1,256]{4,3,2,1,0:T(2,128)(2,1)S(1)}, u32[]{:S(2)}, u32[]{:S(2)}) collective-permute-start(bf16[1,4,26,1,256]{4,3,2,1,0:T(2,128)(2,1)S(1)} %get-tuple-element.30), channel_id=1, source_target_pairs={{0,1},{2,3},{4,5},{6,7},{8,9},{10,11},{12,13},{14,15},{16,17},{18,... | collective-permute-start | bytes 159752 | tf_op jit(solution)/shard_map/ppermute | solution.py:21
  141.2 9.1 %collective-permute-start.7 = (bf16[1,4,26,1,256]{4,3,2,1,0:T(2,128)(2,1)S(1)}, bf16[1,4,26,1,256]{4,3,2,1,0:T(2,128)(2,1)S(1)}, u32[]{:S(2)}, u32[]{:S(2)}) collective-permute-start(bf16[1,4,26,1,256]{4,3,2,1,0:T(2,128)(2,1)S(1)} %get-tuple-element.31), channel_id=1, source_target_pairs={{1,0},{3,2},{5,4},{7,6},{9,8},{11,10},{13,12},{15,14},{17,16},{19,... | collective-permute-start | bytes 159752 | tf_op jit(solution)/shard_map/ppermute | solution.py:24
  152.8 4.2 %copy-start.2 = (bf16[6,26,24,768]{3,2,1,0:T(8,128)(2,1)}, bf16[6,26,24,768]{3,2,1,0:T(8,128)(2,1)S(1)}, u32[]{:S(2)}) copy-start(bf16[6,26,24,768]{3,2,1,0:T(8,128)(2,1)S(1)} %select_maximum_fusion) | copy-start | bytes 17252356
  244.8 2.2 copy-start.5

commit v3 on v2

--- a/solution.py
+++ b/solution.py
@@ -73,7 +73,7 @@
             first = pl.multiple_of((9 * a + 3 * b) * ch, 128)
             term = lax.dot_general(
                 block,
-                weight[:, pl.ds(first, 3 * ch)],
+                weight[:, :, :, pl.ds(first, 3 * ch)].reshape(ch, 3 * ch),
                 NT,
                 preferred_element_type=jnp.float32,
             )
@@ -87,18 +87,28 @@
 def enter(sizes):
     barrier = pltpu.get_barrier_semaphore()
     count = 0
-    for axis, size in sizes.items():
-        me = lax.axis_index(axis)
+    for name in ("lo", "hi", "ty", "tz"):
+        me, size, device = place(sizes, name)
         for d in range(1, size):
             pl.semaphore_signal(
-                barrier, inc=1, device_id={axis: lax.rem(me + d, size)}, device_id_type=MESH
+                barrier, inc=1, device_id=device(lax.rem(me + d, size)), device_id_type=MESH
             )
             count += 1
     pl.semaphore_wait(barrier, count)
 
 
-def fan_out(axis, size, source, target, send, recv):
-    me = lax.axis_index(axis)
+def place(sizes, name):
+    if name == "lo":
+        dp = lax.axis_index("dp")
+        return lax.rem(dp, 2), 2, lambda peer: {"dp": 2 * (dp // 2) + peer}
+    if name == "hi":
+        dp = lax.axis_index("dp")
+        return dp // 2, sizes["dp"] // 2, lambda peer: {"dp": 2 * peer + lax.rem(dp, 2)}
+    return lax.axis_index(name), sizes[name], lambda peer: {name: peer}
+
+
+def fan_out(sizes, name, source, target, send, recv):
+    me, size, device = place(sizes, name)
     copies = []
     for d in range(1, size):
         peer = lax.rem(me + d, size)
@@ -108,7 +118,7 @@
                 dst_ref=target(d),
                 send_sem=send.at[d],
                 recv_sem=recv.at[d],
-                device_id={axis: peer},
+                device_id=device(peer),
                 device_id_type=MESH,
             )
         )
@@ -118,43 +128,37 @@
 
 
 def gather_stages(sizes, shard, whole, sems, first, width, over_tiles):
-    ndp, nty, ntz = sizes["dp"], sizes["ty"], sizes["tz"]
-    dp, ty, tz = lax.axis_index("dp"), lax.axis_index("ty"), lax.axis_index("tz")
-    rows = shard.shape[0]
+    nty, ntz = sizes["ty"], sizes["tz"]
+    ty, tz = lax.axis_index("ty"), lax.axis_index("tz")
+    hi, lo = place(sizes, "hi")[0], place(sizes, "lo")[0]
     span = width // nty
     part = span // ntz if over_tiles else span
     start = first + ty * span
     group = pl.ds(pl.multiple_of(start, 128), span)
     mine = pl.ds(pl.multiple_of(start + tz * part, 128), part) if over_tiles else group
-    own = pl.ds(pl.multiple_of(dp * rows, 16), rows)
-
-    whole[own, mine] = shard[:, mine]
-    copies = fan_out(
-        "dp", ndp, lambda peer: shard.at[:, mine], lambda d: whole.at[own, mine], sems.at[0], sems.at[1]
-    )
-    yield
-    for copy in copies:
-        copy.wait()
+
+    whole[hi, lo, :, mine] = shard[:, mine]
+    steps = [
+        ("hi", shard.at[:, mine], whole.at[hi, lo, :, mine]),
+        ("lo", whole.at[:, lo, :, mine], whole.at[:, lo, :, mine]),
+    ]
     if over_tiles:
+        steps.append(("tz", whole.at[:, :, :, mine], whole.at[:, :, :, mine]))
+    steps.append(("ty", whole.at[:, :, :, group], whole.at[:, :, :, group]))
+    for n, (name, source, target) in enumerate(steps):
         copies = fan_out(
-            "tz", ntz, lambda peer: whole.at[:, mine], lambda d: whole.at[:, mine], sems.at[2], sems.at[3]
+            sizes, name, lambda peer: source, lambda d: target, sems.at[2 * n], sems.at[2 * n + 1]
         )
         yield
         for copy in copies:
             copy.wait()
-    copies = fan_out(
-        "ty", nty, lambda peer: whole.at[:, group], lambda d: whole.at[:, group], sems.at[4], sems.at[5]
-    )
-    yield
-    for copy in copies:
-        copy.wait()
 
 
 def added(count, own, others, store):
     def step(t, _):
         total = own(t).astype(jnp.float32)
         for d in range(others.shape[0]):
-            total += others[d, t].astype(jnp.float32)
+            total += others[d, t].astype(jnp.float32).reshape(total.shape)
         store(t, total)
         return 0
 
@@ -162,73 +166,68 @@
 
 
 def reduce_stages(sizes, part, out, bufs, sems, first, tz_first):
-    ndp, nty, ntz = sizes["dp"], sizes["ty"], sizes["tz"]
-    dp, ty, tz = lax.axis_index("dp"), lax.axis_index("ty"), lax.axis_index("tz")
-    over_ty, sum_ty, over_tz, second, over_dp = bufs
-    wide, rows = sum_ty.shape[0], over_dp.shape[2]
+    nty, ntz = sizes["ty"], sizes["tz"]
+    ty, tz = lax.axis_index("ty"), lax.axis_index("tz")
+    hi, lo = place(sizes, "hi")[0], place(sizes, "lo")[0]
+    over_ty, sum_ty, over_tz, sum_tz, over_lo, sum_lo, over_hi = bufs
+    wide = sum_ty.shape[0]
     few = wide // ntz
     begin = first + ty * wide
     slot = begin + tz * few
-    own = pl.ds(pl.multiple_of(dp * rows, 16), rows)
-
-    def rows_of(peer):
-        return pl.ds(pl.multiple_of(peer * rows, 16), rows)
 
     def put(target, offset):
         def store(t, total):
-            target[offset + t] = total.astype(target.dtype)
+            target[offset + t] = total.reshape(target.shape[1:]).astype(target.dtype)
 
         return store
 
-    copies = fan_out(
-        "ty", nty, lambda peer: part.at[pl.ds(first + peer * wide, wide)], lambda d: over_ty.at[d - 1],
-        sems.at[0], sems.at[1],
+    def send(n, name, source, target):
+        return fan_out(sizes, name, source, target, sems.at[2 * n], sems.at[2 * n + 1])
+
+    copies = send(
+        0, "ty", lambda peer: part.at[pl.ds(first + peer * wide, wide)], lambda d: over_ty.at[d - 1]
     )
     yield
     for copy in copies:
         copy.wait()
     added(wide, lambda t: part[begin + t], over_ty, put(sum_ty, 0))
+    held, count = sum_ty, wide
     if tz_first:
-        copies = fan_out(
-            "tz", ntz, lambda peer: sum_ty.at[pl.ds(peer * few, few)], lambda d: over_tz.at[d - 1],
-            sems.at[2], sems.at[3],
+        copies = send(
+            1, "tz", lambda peer: sum_ty.at[pl.ds(peer * few, few)], lambda d: over_tz.at[d - 1]
         )
         yield
         for copy in copies:
             copy.wait()
-        added(few, lambda t: sum_ty[tz * few + t], over_tz, put(second, 0))
-        copies = fan_out(
-            "dp", ndp, lambda peer: second.at[:, rows_of(peer)], lambda d: over_dp.at[d - 1],
-            sems.at[4], sems.at[5],
+        added(few, lambda t: sum_ty[tz * few + t], over_tz, put(sum_tz, 0))
+        held, count = sum_tz, few
+    copies = send(2, "lo", lambda peer: held.at[:, :, peer], lambda d: over_lo.at[d - 1])
+    yield
+    for copy in copies:
+        copy.wait()
+    added(count, lambda t: held[t, :, lo], over_lo, put(sum_lo, 0))
+    copies = send(3, "hi", lambda peer: sum_lo.at[:, peer], lambda d: over_hi.at[d - 1])
+    yield
+    for copy in copies:
+        copy.wait()
+    if tz_first:
+        added(few, lambda t: sum_lo[t, hi], over_hi, put(out, slot))
+    else:
+        added(wide, lambda t: sum_lo[t, hi], over_hi, put(sum_tz, 0))
+        copies = send(
+            1, "tz", lambda peer: sum_tz.at[pl.ds(peer * few, few)], lambda d: over_tz.at[d - 1]
         )
         yield
         for copy in copies:
             copy.wait()
-        added(few, lambda t: second[t, own], over_dp, put(out, slot))
-    else:
-        copies = fan_out(
-            "dp", ndp, lambda peer: sum_ty.at[:, rows_of(peer)], lambda d: over_dp.at[d - 1],
-            sems.at[4], sems.at[5],
-        )
-        yield
-        for copy in copies:
-            copy.wait()
-        added(wide, lambda t: sum_ty[t, own], over_dp, put(second, 0))
-        copies = fan_out(
-            "tz", ntz, lambda peer: second.at[pl.ds(peer * few, few)], lambda d: over_tz.at[d - 1],
-            sems.at[2], sems.at[3],
-        )
-        yield
-        for copy in copies:
-            copy.wait()
-        added(few, lambda t: second[tz * few + t], over_tz, put(out, slot))
+        added(few, lambda t: sum_tz[tz * few + t], over_tz, put(out, slot))
     mine = out.at[pl.ds(slot, few)]
-    copies = fan_out("tz", ntz, lambda peer: mine, lambda d: mine, sems.at[6], sems.at[7])
+    copies = send(4, "tz", lambda peer: mine, lambda d: mine)
     yield
     for copy in copies:
         copy.wait()
     group = out.at[pl.ds(begin, wide)]
-    copies = fan_out("ty", nty, lambda peer: group, lambda d: group, sems.at[8], sems.at[9])
+    copies = send(5, "ty", lambda peer: group, lambda d: group)
     yield
     for copy in copies:
         copy.wait()
@@ -283,7 +282,7 @@
         first = 0
         for n, (slots, after, tz_first) in enumerate(chains_of(sizes["ty"] * sizes["tz"])):
             if after == b:
-                bufs = refs[5 * n : 5 * n + 5]
+                bufs = refs[7 * n : 7 * n + 7]
                 reductions += advance(
                     [reduce_stages(sizes, terms, reduced, bufs, reduce_sems.at[n], first, tz_first)]
                 )
@@ -333,23 +332,26 @@
 
     chains = chains_of(tiles)
     most = max(sizes.values())
+    highs = ndp // 2
     scratch = [
         pltpu.VMEM((taps, ch, ch), half),
-        pltpu.VMEM((ch, lanes), half),
+        pltpu.VMEM((highs, 2, share, lanes), half),
         pltpu.VMEM((plane, ch), jnp.float32),
         dma((count,)),
-        dma((2, 6, most)),
-        dma((len(chains), 10, most)),
+        dma((2, 8, most)),
+        dma((len(chains), 12, most)),
     ]
     for slots, _, tz_first in chains:
         across = slots // nty
         little = across // ntz
         scratch += [
             pltpu.VMEM((nty - 1, across, ch, ch), half),
-            pltpu.VMEM((across, ch, ch), half),
-            pltpu.VMEM((ntz - 1, little, ch if tz_first else share, ch), half),
-            pltpu.VMEM((little, ch, ch) if tz_first else (across, share, ch), half),
-            pltpu.VMEM((ndp - 1, little if tz_first else across, share, ch), half),
+            pltpu.VMEM((across, highs, 2, share, ch), half),
+            pltpu.VMEM((ntz - 1, little, *((highs, 2) if tz_first else ()), share, ch), half),
+            pltpu.VMEM((little, highs, 2, share, ch) if tz_first else (across, share, ch), half),
+            pltpu.VMEM((1, little if tz_first else across, highs, share, ch), half),
+            pltpu.VMEM((little if tz_first else across, highs, share, ch), half),
+            pltpu.VMEM((highs - 1, little if tz_first else across, share, ch), half),
         ]
     anywhere = pl.BlockSpec(memory_space=pl.ANY)
 

time: 249 us -> 231 us (0.928)
  Pallas kernels: 174 us -> 157 us
    pallas_call x2, Pallas kernels: 174 us -> 157 us  [layer(): pl.pallas_call(functools.partial(layer_kernel, sizes, wide, count, masked...]
where the time goes in v3:
time: 231 us
  Pallas kernels  157 us (68%)
  local copies, waits for them, and re-layouts  32.7 us (14%)
  starting transfers between devices  17.6 us (8%)
  other arithmetic  15.5 us (7%)
  waiting for transfers between devices  6.9 us (3%)
    pallas_call x2, Pallas kernels, layer(): pl.pallas_call(functools.partial(layer_kernel, sizes, wide, count, masked...  157 us
    slice x4, local copies, waits for them, and re-layouts, shifted_views(): lanes[:, 1:1 + high].reshape(depth + 2, high * wide, -1)  13.9 us
    ppermute x4, starting transfers between devices, extended(): lax.ppermute(lax.slice_in_dim(block, block.shape[dim] - width, None, axis...  12.5 us
    ppermute x4, waiting for transfers between devices, extended(): lax.ppermute(lax.slice_in_dim(block, 0, width, axis=dim), axis, backward)  6.78 us
    ppermute x4, starting transfers between devices, extended(): lax.ppermute(lax.slice_in_dim(block, 0, width, axis=dim), axis, backward)  5.16 us
    concatenate x1, other arithmetic, extended(): block = jnp.concatenate([low, block, high], axis=dim)  4.76 us
    unnamed x23, local copies, waits for them, and re-layouts  4.76 us
  transfers between devices with their start and end apart: 8, of which 3 were waited for; matrix products, arithmetic and copies ran while one was open for 7% of the time, Pallas kernels for 0%

profile of v3, /device:TPU:0, one launch (start us, length us, event | category | flops | bytes accessed | tf_op | source)
XLA Modules:
  0.0 230.9 jit_solution(2681986385645018530)
XLA Ops:
  0.6 2.3 compare_select_fusion
  2.9 0.0 copy-done.4
  3.0 2.4 %collective-permute-start = (bf16[3,4,1,24,256]{4,3,2,1,0:T(8,128)(2,1)S(1)}, bf16[3,4,1,24,256]{4,3,2,1,0:T(8,128)(2,1)S(1)}, u32[]{:S(2)}, u32[]{:S(2)}) collective-permute-start(bf16[3,4,1,24,256]{4,3,2,1,0:T(8,128)(2,1)S(1)} %get-tuple-element.16), channel_id=1, source_target_pairs={{0,2},{1,3},{4,6},{5,7},{8,10},{9,11},{12,14},{13,15},{16,18},{17,... | collective-permute-start | bytes 442376 | tf_op jit(solution)/shard_map/ppermute | solution.py:21
  5.4 1.3 collective-permute-start.1
  6.7 0.0 collective-permute-done
  6.7 1.9 collective-permute-done.1
  8.6 1.4 pad_maximum_fusion.5
  10.1 5.0 %collective-permute-start.2 = (bf16[3,4,26,1,256]{4,3,2,1,0:T(2,128)(2,1)}, bf16[3,4,26,1,256]{4,3,2,1,0:T(2,128)(2,1)}, u32[]{:S(2)}, u32[]{:S(2)}) collective-permute-start(bf16[3,4,26,1,256]{4,3,2,1,0:T(2,128)(2,1)} %get-tuple-element.14), channel_id=1, source_target_pairs={{0,1},{2,3},{4,5},{6,7},{8,9},{10,11},{12,13},{14,15},{16,17},{18,... | collective-permute-start | bytes 479240 | tf_op jit(solution)/shard_map/ppermute | solution.py:21
  15.0 1.3 collective-permute-start.3
  16.3 1.5 copy.15
  17.9 1.1 copy.21
  19.0 1.0 copy.22
  20.0 0.8 pad.23.refs_5_
  20.8 0.8 pad.25.refs_5_
  21.6 0.1 collective-permute-done.2
  21.7 4.8 %collective-permute-done.3 = bf16[3,4,26,1,256]{4,3,2,1,0:T(2,128)(2,1)} collective-permute-done((bf16[3,4,26,1,256]{4,3,2,1,0:T(2,128)(2,1)}, bf16[3,4,26,1,256]{4,3,2,1,0:T(2,128)(2,1)}, u32[]{:S(2)}, u32[]{:S(2)}) %collective-permute-start.3) | collective-permute-done | bytes 159776 | tf_op jit(solution)/shard_map/ppermute | solution.py:24
  26.6 4.8 %pad_maximum_fusion = bf16[3,4,26,26,256]{4,3,2,1,0:T(8,128)(2,1)S(1)} fusion(bf16[3,4,26,1,256]{4,3,2,1,0:T(2,128)(2,1)} %collective-permute-done.3, bf16[3,4,1,24,256]{4,3,2,1,0:T(8,128)(2,1)S(1)} %copy-done.9, bf16[1,4,24,24,256]{4,3,2,1,0:T(8,128)(2,1)S(1)} %copy-done.4, bf16[1,4,24,24,256]{4,3,2,1,0:T(8,128)(2,1)S(1)} %get-tuple-element.35, ...), kind=kLoop, calls=%fused_computation.11 | loop fusion | flops 29073408 | bytes 8306688 | tf_op jit(solution)/shard_map/concatenate | solution.py:25
  31.3 0.6 slice_bitcast_fusion
  32.0 0.9 fusion.2
  32.9 0.4 select_maximum_fusion.2
  33.4 2.9 %slice.130 = bf16[6,24,24,768]{3,2,1,0:T(8,128)(2,1)} slice(bf16[6,26,24,768]{3,2,1,0:T(8,128)(2,1)S(1)} %select_maximum_fusion.2), slice={[0:6], [1:25], [0:24], [0:768]} | slice | bytes 10616832 | tf_op jit(solution)/shard_map/slice | solution.py:37
  36.3 1.3 copy-done
  37.6 1.0 fusion.3
  38.5 0.4 select_maximum_fusion.4
  39.0 2.9 %slice.125 = bf16[6,24,24,768]{3,2,1,0:T(8,128)(2,1)} slice(bf16[6,26,24,768]{3,2,1,0:T(8,128)(2,1)S(1)} %select_maximum_fusion.4), slice={[0:6], [1:25], [0:24], [0:768]} | slice | bytes 10616832 | tf_op jit(solution)/shard_map/slice | solution.py:37
  41.9 1.2 copy-done.1
  43.1 76.3 %second_layer.1 = (bf16[4,576,256]{2,1,0:T(8,128)(2,1)}, bf16[28,32,256]{2,1,0:T(8,128)(2,1)}) custom-call(bf16[6,624,768]{2,1,0:T(8,128)(2,1)} %bitcast.36, bf16[6,576,768]{2,1,0:T(8,128)(2,1)} %bitcast.42, bf16[6,624,768]{2,1,0:T(8,128)(2,1)} %bitcast.35, bf16[6,576,768]{2,1,0:T(8,128)(2,1)} %bitcast.41, bf16[256,2304]{1,0:T(8,128)(2,1)} %bitcast.48, ...), custom_call_target="tpu_custom_call" | custom-call | tf_op jit(solution)/shard_map/second_layer/pallas_call | solution.py:365
  119.4 0.8 fusion.5
  120.2 2.2 collective-permute-start.4
  122.5 1.3 collective-permute-start.5
  123.8 0.9 fusion.4
  124.7 3.0 %select_maximum_fusion.6 = bf16[6,26,24,768]{3,2,1,0:T(8,128)(2,1)} fusion(bf16[4,26,24,256]{3,2,1,0:T(8,128)(2,1)S(1)} %get-tuple-element.28, bf16[4,26,24,256]{3,2,1,0:T(8,128)(2,1)S(1)} %get-tuple-element.29, bf16[4,26,24,256]{3,2,1,0:T(8,128)(2,1)S(1)} %get-tuple-element.27), kind=kLoop, calls=%fused_computation.9 | loop fusion | flops 34504704 | bytes 9584640 | tf_op jit(solution)/shard_map/concatenate | solution.py:32
  127.7 0.2 pad_maximum_fusion.11
  127.9 2.9 %collective-permute-start.6 = (bf16[1,4,26,1,256]{4,3,2,1,0:T(2,128)(2,1)S(1)}, bf16[1,4,26,1,256]{4,3,2,1,0:T(2,128)(2,1)S(1)}, u32[]{:S(2)}, u32[]{:S(2)}) collective-permute-start(bf16[1,4,26,1,256]{4,3,2,1,0:T(2,128)(2,1)S(1)} %get-tuple-element.30), channel_id=1, source_target_pairs={{0,1},{2,3},{4,5},{6,7},{8,9},{10,11},{12,13},{14,15},{16,17},{18,... | collective-permute-start | bytes 159752 | tf_op jit(solution)/shard_map/ppermute | solution.py:21
  130.8 1.3 collective-permute-start.7
  132.1 0.1 convert_multiply_fusion
  132.2 1.5 copy.17
  133.7 5.1 %slice.120 = bf16[6,24,24,768]{3,2,1,0:T(8,128)(2,1)} slice(bf16[6,26,24,768]{3,2,1,0:T(8,128)(2,1)} %select_maximum_fusion.6), slice={[0:6], [1:25], [0:24], [0:768]} | slice | bytes 10616832 | tf_op jit(solution)/shard_map/slice | solution.py:37
  138.9 1.0 copy.20
  139.9 1.2 maximum_bitcast_fusion
  141.0 0.9 fusion.1
  142.0 0.4 select_maximum_fusion
  142.4 2.9 %slice.136 = bf16[6,24,24,768]{3,2,1,0:T(8,128)(2,1)} slice(bf16[6,26,24,768]{3,2,1,0:T(8,128)(2,1)S(1)} %select_maximum_fusion), slice={[0:6], [1:25], [0:24], [0:768]} | slice | bytes 10616832 | tf_op jit(solution)/shard_map/slice | solution.py:37
  145.3 1.3 copy-done.2
  146.6 81.0 %first_layer.1 = (bf16[4,576,256]{2,1,0:T(8,128)(2,1)}, bf16[28,32,256]{2,1,0:T(8,128)(2,1)}) custom-call(bf16[6,624,768]{2,1,0:T(8,128)(2,1)} %bitcast.37, bf16[6,576,768]{2,1,0:T(8,128)(2,1)} %bitcast.40, bf16[6,624,768]{2,1,0:T(8,128)(2,1)} %bitcast.38, bf16[6,576,768]{2,1,0:T(8,128)(2,1)} %bitcast.43, bf16[256,2304]{1,0:T(8,128)(2,1)} %bitcast.49, ...), custom_call_target="tpu_custom_call" | custom-call | tf_op jit(solution)/shard_map/first_layer/pallas_call | solution.py:365
  227.6 1.2 convert_multiply_fusion.1
  228.8 1.0 copy.19
  229.9 1.0 copy.24
  (23 shorter events, 0.1 us)
Async XLA Ops:
  0.6 2.3 %copy-start.4 = (bf16[1,4,24,24,256]{4,3,2,1,0:T(8,128)(2,1)S(1)}, bf16[1,4,24,24,256]{4,3,2,1,0:T(8,128)(2,1)}, u32[]{:S(2)}) copy-start(bf16[1,4,24,24,256]{4,3,2,1,0:T(8,128)(2,1)} %param.6) | copy-start | bytes 3538948
  3.0 3.7 %collective-permute-start = (bf16[3,4,1,24,256]{4,3,2,1,0:T(8,128)(2,1)S(1)}, bf16[3,4,1,24,256]{4,3,2,1,0:T(8,128)(2,1)S(1)}, u32[]{:S(2)}, u32[]{:S(2)}) collective-permute-start(bf16[3,4,1,24,256]{4,3,2,1,0:T(8,128)(2,1)S(1)} %get-tuple-element.16), channel_id=1, source_target_pairs={{0,2},{1,3},{4,6},{5,7},{8,10},{9,11},{12,14},{13,15},{16,18},{17,... | collective-permute-start | bytes 442376 | tf_op jit(solution)/shard_map/ppermute | solution.py:21
  5.4 3.3 %collective-permute-start.1 = (bf16[3,4,1,24,256]{4,3,2,1,0:T(8,128)(2,1)S(1)}, bf16[3,4,1,24,256]{4,3,2,1,0:T(8,128)(2,1)S(1)}, u32[]{:S(2)}, u32[]{:S(2)}) collective-permute-start(bf16[3,4,1,24,256]{4,3,2,1,0:T(8,128)(2,1)S(1)} %get-tuple-element.17), channel_id=1, source_target_pairs={{2,0},{3,1},{6,4},{7,5},{10,8},{11,9},{14,12},{15,13},{18,16},{19,... | collective-permute-start | bytes 442376 | tf_op jit(solution)/shard_map/ppermute | solution.py:24
  6.7 2.0 copy-start.6
  8.6 1.4 copy-start.8
  10.1 11.6 %collective-permute-start.2 = (bf16[3,4,26,1,256]{4,3,2,1,0:T(2,128)(2,1)}, bf16[3,4,26,1,256]{4,3,2,1,0:T(2,128)(2,1)}, u32[]{:S(2)}, u32[]{:S(2)}) collective-permute-start(bf16[3,4,26,1,256]{4,3,2,1,0:T(2,128)(2,1)} %get-tuple-element.14), channel_id=1, source_target_pairs={{0,1},{2,3},{4,5},{6,7},{8,9},{10,11},{12,13},{14,15},{16,17},{18,... | collective-permute-start | bytes 479240 | tf_op jit(solution)/shard_map/ppermute | solution.py:21
  15.0 11.5 %collective-permute-start.3 = (bf16[3,4,26,1,256]{4,3,2,1,0:T(2,128)(2,1)}, bf16[3,4,26,1,256]{4,3,2,1,0:T(2,128)(2,1)}, u32[]{:S(2)}, u32[]{:S(2)}) collective-permute-start(bf16[3,4,26,1,256]{4,3,2,1,0:T(2,128)(2,1)} %get-tuple-element.15), channel_id=1, source_target_pairs={{1,0},{3,2},{5,4},{7,6},{9,8},{11,10},{13,12},{15,14},{17,16},{19,... | collective-permute-start | bytes 479240 | tf_op jit(solution)/shard_map/ppermute | solution.py:24
  17.9 8.7 %copy-start.7 = (bf16[3,4,1,24,256]{4,3,2,1,0:T(8,128)(2,1)S(1)}, bf16[3,4,1,24,256]{4,3,2,1,0:T(8,128)(2,1)}, u32[]{:S(2)}) copy-start(bf16[3,4,1,24,256]{4,3,2,1,0:T(8,128)(2,1)} %copy-done.6) | copy-start | bytes 442372
  17.9 8.7 %copy-start.9 = (bf16[3,4,1,24,256]{4,3,2,1,0:T(8,128)(2,1)S(1)}, bf16[3,4,1,24,256]{4,3,2,1,0:T(8,128)(2,1)}, u32[]{:S(2)}) copy-start(bf16[3,4,1,24,256]{4,3,2,1,0:T(8,128)(2,1)} %copy-done.8) | copy-start | bytes 442372
  33.4 4.2 %copy-start = (bf16[6,26,24,768]{3,2,1,0:T(8,128)(2,1)}, bf16[6,26,24,768]{3,2,1,0:T(8,128)(2,1)S(1)}, u32[]{:S(2)}) copy-start(bf16[6,26,24,768]{3,2,1,0:T(8,128)(2,1)S(1)} %select_maximum_fusion.2) | copy-start | bytes 17252356
  39.0 4.1 %copy-start.1 = (bf16[6,26,24,768]{3,2,1,0:T(8,128)(2,1)}, bf16[6,26,24,768]{3,2,1,0:T(8,128)(2,1)S(1)}, u32[]{:S(2)}) copy-start(bf16[6,26,24,768]{3,2,1,0:T(8,128)(2,1)S(1)} %select_maximum_fusion.4) | copy-start | bytes 17252356
  120.2 7.5 %collective-permute-start.4 = (bf16[1,4,1,24,256]{4,3,2,1,0:T(8,128)(2,1)S(1)}, bf16[1,4,1,24,256]{4,3,2,1,0:T(8,128)(2,1)S(1)}, u32[]{:S(2)}, u32[]{:S(2)}) collective-permute-start(bf16[1,4,1,24,256]{4,3,2,1,0:T(8,128)(2,1)S(1)} %get-tuple-element.32), channel_id=1, source_target_pairs={{0,2},{1,3},{4,6},{5,7},{8,10},{9,11},{12,14},{13,15},{16,18},{17,... | collective-permute-start | bytes 147464 | tf_op jit(solution)/shard_map/ppermute | solution.py:21
  122.5 5.2 %collective-permute-start.5 = (bf16[1,4,1,24,256]{4,3,2,1,0:T(8,128)(2,1)S(1)}, bf16[1,4,1,24,256]{4,3,2,1,0:T(8,128)(2,1)S(1)}, u32[]{:S(2)}, u32[]{:S(2)}) collective-permute-start(bf16[1,4,1,24,256]{4,3,2,1,0:T(8,128)(2,1)S(1)} %get-tuple-element.33), channel_id=1, source_target_pairs={{2,0},{3,1},{6,4},{7,5},{10,8},{11,9},{14,12},{15,13},{18,16},{19,... | collective-permute-start | bytes 147464 | tf_op jit(solution)/shard_map/ppermute | solution.py:24
  124.7 3.0 %copy-start.3 = (bf16[4,576,256]{2,1,0:T(8,128)(2,1)S(1)}, bf16[4,576,256]{2,1,0:T(8,128)(2,1)}, u32[]{:S(2)}) copy-start(bf16[4,576,256]{2,1,0:T(8,128)(2,1)} %get-tuple-element.7) | copy-start | bytes 3538948
  124.7 7.4 %copy-start.10 = (bf16[28,32,256]{2,1,0:T(8,128)(2,1)S(1)}, bf16[28,32,256]{2,1,0:T(8,128)(2,1)}, u32[]{:S(2)}) copy-start(bf16[28,32,256]{2,1,0:T(8,128)(2,1)} %get-tuple-element.10) | copy-start | bytes 1376260
  127.9 12.0 %collective-permute-start.6 = (bf16[1,4,26,1,256]{4,3,2,1,0:T(2,128)(2,1)S(1)}, bf16[1,4,26,1,256]{4,3,2,1,0:T(2,128)(2,1)S(1)}, u32[]{:S(2)}, u32[]{:S(2)}) collective-permute-start(bf16[1,4,26,1,256]{4,3,2,1,0:T(2,128)(2,1)S(1)} %get-tuple-element.30), channel_id=1, source_target_pairs={{0,1},{2,3},{4,5},{6,7},{8,9},{10,11},{12,13},{14,15},{16,17},{18,... | collective-permute-start | bytes 159752 | tf_op jit(solution)/shard_map/ppermute | solution.py:21
  130.8 9.1 %collective-permute-start.7 = (bf16[1,4,26,1,256]{4,3,2,1,0:T(2,128)(2,1)S(1)}, bf16[1,4,26,1,256]{4,3,2,1,0:T(2,128)(2,1)S(1)}, u32[]{:S(2)}, u32[]{:S(2)}) collective-permute-start(bf16[1,4,26,1,256]{4,3,2,1,0:T(2,128)(2,1)S(1)} %get-tuple-element.31), channel_id=1, source_target_pairs={{1,0},{3,2},{5,4},{7,6},{9,8},{11,10},{13,12},{15,14},{17,16},{19,... | collective-permute-start | bytes 159752 | tf_op jit(solution)/shard_map/ppermute | solution.py:24
  142.4 4.2 %copy-start.2 = (bf16[6,26,24,768]{3,2,1,0:T(8,128)(2,1)}, bf16[6,26,24,768]{3,2,1,0:T(8,128)(2,1)S(1)}, u32[]{:S(2)}) copy-start(bf16[6,26,24,768]{3,2,1,0:T(8,128)(2,1)S(1)} %select_maximum_fusion) | copy-start | bytes 17252356
  227.6 2.2 copy-start.5
